TPU v7x, 512 devices: a whole 4x4x16 slice. The times are simulated.
512 devices in a mesh: gx: 64 (over y, z), gy: 8 (over x, core).
Axes of the slice: x: 4, y: 4, z: 16, core: 2. Of those that a mesh axis runs over, the one named last changes fastest.
Arguments:
- source: float32 [8, 2048, 2048], P(None, 'gx', 'gy'), may hold values from -6 to 6
- kappa_sq: bfloat16 [8, 2048, 2048], P(None, 'gx', 'gy'), may hold values from 0.0039978027 to 0.079589844
- face_x: bfloat16 [8, 2048, 2048], P(None, 'gx', 'gy'), may hold values from 0.25 to 1
- face_y: bfloat16 [8, 2048, 2048], P(None, 'gx', 'gy'), may hold values from 0.25 to 1
- face_z: bfloat16 [8, 2048, 2048], P(None, 'gx', 'gy'), may hold values from 0.0049743652 to 0.049804688
Outputs:
- field: float32 [8, 2048, 2048], P(None, 'gx', 'gy')
All inputs are finite; a program needn't handle non-finite values.
Results may differ from a plain program's by a relative error of at most 0.0003.
Values sent between devices are 32-bit elements; how exact they have to be, the bound alone decides.
A program may use at most 64 MiB of HBM per device.

v0:
```python
import jax
import jax.numpy as jnp
from jax import lax
from jax.sharding import PartitionSpec as P

LEVELS = 5
COARSE_SWEEPS = 4


DAMPING = 0.8


def padded_2(shard, sides, width):
    for axis, dim in sides:
        size, length = (lax.axis_size(axis), shard.shape[dim])
        up = [(i, (i + 1) % size) for i in range(size - 1)]
        down = [(j, i) for i, j in up]
        last = lax.slice_in_dim(shard, length - width, length, axis=dim)
        initial = lax.slice_in_dim(shard, 0, width, axis=dim)
        before = lax.ppermute(last, axis, up)
        after = lax.ppermute(initial, axis, down)
        shard = jnp.concatenate([before, shard, after], axis=dim)
    return shard


def from_behind(block, axis, distance):
    devices = range(lax.axis_size(axis))
    route = [(i - distance, i) for i in devices if i - distance in devices]
    return lax.ppermute(block, axis, route)


def lower_cells(values, which_axis):
    padded = jnp.pad(
        values, [(1, 0) if dimension == which_axis else (0, 0) for dimension in range(3)]
    )
    return lax.slice_in_dim(padded, 0, values.shape[which_axis], axis=which_axis)


def upper_cells(values, which_axis):
    padded = jnp.pad(
        values, [(0, 1) if dimension == which_axis else (0, 0) for dimension in range(3)]
    )
    return lax.slice_in_dim(padded, 1, values.shape[which_axis] + 1, axis=which_axis)


def restrict(values):
    layer_count, row_count, col_count = values.shape
    blocks = values.astype(jnp.float32).reshape(layer_count, row_count // 2, 2, col_count // 2, 2)
    return (
        blocks[:, :, 0, :, 0]
        + blocks[:, :, 0, :, 1]
        + blocks[:, :, 1, :, 0]
        + blocks[:, :, 1, :, 1]
    ) * 0.25


def coarsen(coefficients):
    kappa_sq, face_x, face_y, face_z = coefficients
    face_x = face_x.astype(jnp.float32)
    face_y = face_y.astype(jnp.float32)
    coarse_x = (face_x[:, 1::2, 0::2] + face_x[:, 1::2, 1::2]) * 0.25
    coarse_y = (face_y[:, 0::2, 1::2] + face_y[:, 1::2, 1::2]) * 0.25
    return (restrict(kappa_sq), coarse_x, coarse_y, restrict(face_z))


def prolong(values):
    return jnp.repeat(jnp.repeat(values, 2, axis=1), 2, axis=2)


def field_rims(values):
    return padded_2(values, (("gx", 1), ("gy", 2)), 1)


def build_level(coefficients, rim_row, rim_col):
    kappa_sq, face_x, face_y, face_z = coefficients
    below_x = jnp.concatenate([rim_row[:, None, :], face_x[:, :-1, :].astype(jnp.float32)], axis=1)
    below_y = jnp.concatenate([rim_col[:, :, None], face_y[:, :, :-1].astype(jnp.float32)], axis=2)
    below_z = lower_cells(face_z, 0)
    diagonal = kappa_sq.astype(jnp.float32) + face_x.astype(jnp.float32) + below_x
    diagonal = diagonal + face_y.astype(jnp.float32) + below_y
    diagonal = diagonal + face_z.astype(jnp.float32) + below_z.astype(jnp.float32)
    return (face_x, below_x, face_y, below_y, face_z, below_z, diagonal)


def apply_padded(padded, level_data):
    face_x, below_x, face_y, below_y, face_z, below_z, diagonal = level_data
    center = padded[:, 1:-1, 1:-1]
    beside_all = face_x * padded[:, 2:, 1:-1] + below_x * padded[:, :-2, 1:-1]
    beside_all = beside_all + face_y * padded[:, 1:-1, 2:] + below_y * padded[:, 1:-1, :-2]
    beside_all = beside_all + face_z * upper_cells(center, 0) + below_z * lower_cells(center, 0)
    return (center, diagonal * center - beside_all)


def sweep_padded(padded, right_side, level_data):
    center, applied = apply_padded(padded, level_data)
    return center + DAMPING * (right_side - applied) / level_data[6]


def solve_level(level_index, right_side, levels):
    level_data = levels[level_index]
    values = DAMPING * right_side / level_data[6]
    if level_index == LEVELS:
        for sweep_index in range(COARSE_SWEEPS - 1):
            values = sweep_padded(field_rims(values), right_side, level_data)
        return values
    smoothed = sweep_padded(field_rims(values), right_side, level_data)
    padded = field_rims(smoothed)
    center, applied = apply_padded(padded, level_data)
    residual = right_side - applied
    correction = solve_level(level_index + 1, restrict(residual), levels)
    corrected = smoothed + prolong(correction)
    padded = field_rims(corrected)
    smoothed = sweep_padded(padded, right_side, level_data)
    return sweep_padded(field_rims(smoothed), right_side, level_data)


def on_device(source, kappa_sq, face_x, face_y, face_z):
    hierarchy = [(kappa_sq, face_x, face_y, face_z)]
    for level_index in range(LEVELS):
        hierarchy.append(coarsen(hierarchy[-1]))
    last_rows = jnp.concatenate(
        [coefficients[1][:, -1, :].astype(jnp.float32) for coefficients in hierarchy], axis=1
    )
    last_cols = jnp.concatenate(
        [coefficients[2][:, :, -1].astype(jnp.float32) for coefficients in hierarchy], axis=1
    )
    rows_below = from_behind(last_rows, "gx", 1)
    cols_before = from_behind(last_cols, "gy", 1)
    levels = []
    offset_row = 0
    offset_col = 0
    for coefficients in hierarchy:
        row_count = coefficients[1].shape[1]
        col_count = coefficients[1].shape[2]
        rim_row = rows_below[:, offset_row : offset_row + col_count]
        rim_col = cols_before[:, offset_col : offset_col + row_count]
        levels.append(build_level(coefficients, rim_row, rim_col))
        offset_row = offset_row + col_count
        offset_col = offset_col + row_count
    return solve_level(0, source, levels)


def solution(mesh):
    placed = (
        P(None, "gx", "gy"),
        P(None, "gx", "gy"),
        P(None, "gx", "gy"),
        P(None, "gx", "gy"),
        P(None, "gx", "gy"),
    )
    return jax.shard_map(
        on_device, mesh=mesh, in_specs=placed, out_specs=P(None, "gx", "gy"), check_vma=False
    )
```

profile of v0, /device:TPU:24, one launch (start us, length us, event | category | flops | bytes accessed | tf_op | source)
XLA Modules:
  0.0 526.1 jit_solution(3552571021678004866)
XLA Ops:
  5.3 3.6 slice.1123
  17.0 3.6 slice.1105
  20.7 3.6 slice.1106
  29.5 3.8 collective-permute-start
  37.1 7.4 %fusion.365 = (f32[8,16,1,128,1]{0,4,3,2,1:T(1,128)S(1)}, f32[8,16,1,128,1]{0,4,3,2,1:T(1,128)}, f32[8,16,1,128,1]{0,4,3,2,1:T(1,128)}, f32[8,16,1,128,1]{0,4,3,2,1:T(1,128)}) fusion(f32[8,16,2,128,2]{0,4,3,2,1:T(2,128)} %bitcast.250), kind=kLoop, calls=%fused_computation.710 | loop fusion | bytes 524288 | tf_op jit(solution)/shard_map/slice | solution.py:51
  54.5 7.4 %fusion.364 = (f32[8,16,1,128,1]{0,4,3,2,1:T(1,128)}, f32[8,16,1,128,1]{0,4,3,2,1:T(1,128)}, f32[8,16,1,128,1]{0,4,3,2,1:T(1,128)}, f32[8,16,1,128,1]{0,4,3,2,1:T(1,128)}) fusion(f32[8,16,2,128,2]{0,4,3,2,1:T(2,128)} %bitcast.251), kind=kLoop, calls=%fused_computation.709 | loop fusion | bytes 524288 | tf_op jit(solution)/shard_map/slice | solution.py:51
  68.5 9.7 %collective-permute-start.2 = (f32[8,1,256]{2,0,1:T(8,128)S(1)}, f32[8,1,256]{2,0,1:T(8,128)S(1)}, u32[]{:S(2)}, u32[]{:S(2)}) collective-permute-start(f32[8,1,256]{2,0,1:T(8,128)S(1)} %get-tuple-element.76), channel_id=1, source_target_pairs={{8,0},{16,8},{24,16},{32,24},{40,32},{48,40},{56,48},{64,56},{72,6... | collective-permute-start | bytes 24584 | tf_op jit(solution)/shard_map/ppermute | solution.py:21
  80.4 5.4 %collective-permute-done.3 = f32[8,1,256]{2,0,1:T(8,128)S(1)} collective-permute-done((f32[8,1,256]{2,0,1:T(8,128)S(1)}, f32[8,1,256]{2,0,1:T(8,128)S(1)}, u32[]{:S(2)}, u32[]{:S(2)}) %collective-permute-start.3) | collective-permute-done | bytes 8224 | tf_op jit(solution)/shard_map/ppermute | solution.py:20
  105.6 3.9 collective-permute-start.7
  125.3 7.5 %fusion.363 = (f32[8,16,1,128,1]{0,4,3,2,1:T(1,128)S(1)}, f32[8,16,1,128,1]{0,4,3,2,1:T(1,128)}, f32[8,16,1,128,1]{0,4,3,2,1:T(1,128)}, f32[8,16,1,128,1]{0,4,3,2,1:T(1,128)}) fusion(f32[8,16,2,128,2]{0,4,3,2,1:T(2,128)} %bitcast.252), kind=kLoop, calls=%fused_computation.708 | loop fusion | bytes 524288 | tf_op jit(solution)/shard_map/slice | solution.py:51
  147.4 3.9 collective-permute-start.11
  155.1 4.4 collective-permute-start.13
  165.9 3.9 collective-permute-start.15
  174.3 4.4 collective-permute-start.17
  217.1 3.8 collective-permute-start.23
  235.5 3.9 collective-permute-start.27
  252.5 3.9 collective-permute-start.31
  269.8 3.9 collective-permute-start.35
  286.5 3.9 collective-permute-start.39
  303.7 3.9 collective-permute-start.43
  307.6 3.7 collective-permute-done.43
  320.4 3.9 collective-permute-start.47
  324.3 3.7 collective-permute-done.47
  337.0 3.9 collective-permute-start.51
  341.0 3.7 collective-permute-done.51
  353.8 3.9 collective-permute-start.55
  357.8 3.7 collective-permute-done.55
  370.5 3.9 collective-permute-start.59
  374.4 3.7 collective-permute-done.59
  387.4 3.9 collective-permute-start.63
  391.3 3.7 collective-permute-done.63
  404.1 3.9 collective-permute-start.67
  408.1 3.7 collective-permute-done.67
  421.2 3.9 collective-permute-start.71
  425.2 3.7 collective-permute-done.71
  438.1 3.9 collective-permute-start.75
  442.0 3.7 collective-permute-done.75
  455.5 3.9 collective-permute-start.79
  459.4 3.7 collective-permute-done.79
  472.6 3.9 collective-permute-start.83
  476.5 3.7 collective-permute-done.83
  480.3 3.8 collective-permute-start.85
  490.7 3.9 collective-permute-start.87
  494.6 3.7 collective-permute-done.87
  498.5 3.8 collective-permute-start.89
  508.7 3.9 collective-permute-start.91
  512.7 3.7 collective-permute-done.91
  516.5 4.4 collective-permute-start.93
  (469 shorter events, 321.3 us)
Async XLA Ops:
  14.3 53.5 %collective-permute-start.1 = (f32[8,63]{1,0:T(8,128)S(1)}, f32[8,63]{1,0:T(8,128)S(1)}, u32[]{:S(2)}, u32[]{:S(2)}) collective-permute-start(f32[8,63]{1,0:T(8,128)S(1)} %concatenate.391), channel_id=1, source_target_pairs={{0,1},{1,2},{2,3},{3,4},{4,5},{5,6},{6,7},{8,9},{9,10},{10,11},{11... | collective-permute-start | bytes 6056 | tf_op jit(solution)/shard_map/ppermute | solution.py:29
  29.5 38.5 %collective-permute-start = (f32[8,504]{1,0:T(8,128)S(1)}, f32[8,504]{1,0:T(8,128)S(1)}, u32[]{:S(2)}, u32[]{:S(2)}) collective-permute-start(f32[8,504]{1,0:T(8,128)S(1)} %concatenate.389), channel_id=1, source_target_pairs={{0,8},{8,16},{16,24},{24,32},{32,40},{40,48},{48,56},{56,64},{64,7... | collective-permute-start | bytes 48392 | tf_op jit(solution)/shard_map/ppermute | solution.py:29
  68.5 11.9 %collective-permute-start.2 = (f32[8,1,256]{2,0,1:T(8,128)S(1)}, f32[8,1,256]{2,0,1:T(8,128)S(1)}, u32[]{:S(2)}, u32[]{:S(2)}) collective-permute-start(f32[8,1,256]{2,0,1:T(8,128)S(1)} %get-tuple-element.76), channel_id=1, source_target_pairs={{8,0},{16,8},{24,16},{32,24},{40,32},{48,40},{56,48},{64,56},{72,6... | collective-permute-start | bytes 24584 | tf_op jit(solution)/shard_map/ppermute | solution.py:21
  78.2 7.7 %collective-permute-start.3 = (f32[8,1,256]{2,0,1:T(8,128)S(1)}, f32[8,1,256]{2,0,1:T(8,128)S(1)}, u32[]{:S(2)}, u32[]{:S(2)}) collective-permute-start(f32[8,1,256]{2,0,1:T(8,128)S(1)} %get-tuple-element.75), channel_id=1, source_target_pairs={{0,8},{8,16},{16,24},{24,32},{32,40},{40,48},{48,56},{56,64},{64,7... | collective-permute-start | bytes 24584 | tf_op jit(solution)/shard_map/ppermute | solution.py:20
  86.6 14.7 %collective-permute-start.5 = (f32[8,34,1]{2,0,1:T(8,128)}, f32[8,34,1]{2,0,1:T(8,128)S(1)}, u32[]{:S(2)}, u32[]{:S(2)}) collective-permute-start(f32[8,34,1]{2,0,1:T(8,128)} %get-tuple-element.56), channel_id=1, source_target_pairs={{0,1},{1,2},{2,3},{3,4},{4,5},{5,6},{6,7},{8,9},{9,10},{10,11},{11... | collective-permute-start | bytes 3272 | tf_op jit(solution)/shard_map/ppermute | solution.py:20
  88.9 13.1 %collective-permute-start.4 = (f32[8,34,1]{2,0,1:T(8,128)}, f32[8,34,1]{2,0,1:T(8,128)}, u32[]{:S(2)}, u32[]{:S(2)}) collective-permute-start(f32[8,34,1]{2,0,1:T(8,128)} %get-tuple-element.55), channel_id=1, source_target_pairs={{1,0},{2,1},{3,2},{4,3},{5,4},{6,5},{7,6},{9,8},{10,9},{11,10},{12... | collective-permute-start | bytes 3272 | tf_op jit(solution)/shard_map/ppermute | solution.py:21
  103.6 7.4 %collective-permute-start.6 = (f32[8,1,256]{2,0,1:T(8,128)S(1)}, f32[8,1,256]{2,0,1:T(8,128)S(1)}, u32[]{:S(2)}, u32[]{:S(2)}) collective-permute-start(f32[8,1,256]{2,0,1:T(8,128)S(1)} %get-tuple-element.74), channel_id=1, source_target_pairs={{8,0},{16,8},{24,16},{32,24},{40,32},{48,40},{56,48},{64,56},{72,6... | collective-permute-start | bytes 24584 | tf_op jit(solution)/shard_map/ppermute | solution.py:21
  105.6 7.7 %collective-permute-start.7 = (f32[8,1,256]{2,0,1:T(8,128)S(1)}, f32[8,1,256]{2,0,1:T(8,128)S(1)}, u32[]{:S(2)}, u32[]{:S(2)}) collective-permute-start(f32[8,1,256]{2,0,1:T(8,128)S(1)} %get-tuple-element.73), channel_id=1, source_target_pairs={{0,8},{8,16},{16,24},{24,32},{32,40},{40,48},{48,56},{56,64},{64,7... | collective-permute-start | bytes 24584 | tf_op jit(solution)/shard_map/ppermute | solution.py:20
  145.5 6.6 %collective-permute-start.10 = (f32[8,1,128]{2,0,1:T(8,128)S(1)}, f32[8,1,128]{2,0,1:T(8,128)S(1)}, u32[]{:S(2)}, u32[]{:S(2)}) collective-permute-start(f32[8,1,128]{2,0,1:T(8,128)S(1)} %get-tuple-element.110), channel_id=1, source_target_pairs={{8,0},{16,8},{24,16},{32,24},{40,32},{48,40},{56,48},{64,56},{72,6... | collective-permute-start | bytes 12296 | tf_op jit(solution)/shard_map/ppermute | solution.py:21
  147.4 7.6 %collective-permute-start.11 = (f32[8,1,128]{2,0,1:T(8,128)S(1)}, f32[8,1,128]{2,0,1:T(8,128)S(1)}, u32[]{:S(2)}, u32[]{:S(2)}) collective-permute-start(f32[8,1,128]{2,0,1:T(8,128)S(1)} %get-tuple-element.109), channel_id=1, source_target_pairs={{0,8},{8,16},{16,24},{24,32},{32,40},{40,48},{48,56},{56,64},{64,7... | collective-permute-start | bytes 12296 | tf_op jit(solution)/shard_map/ppermute | solution.py:20
  155.1 7.8 %collective-permute-start.13 = (f32[8,18,1]{2,0,1:T(8,128)S(1)}, f32[8,18,1]{2,0,1:T(8,128)S(1)}, u32[]{:S(2)}, u32[]{:S(2)}) collective-permute-start(f32[8,18,1]{2,0,1:T(8,128)S(1)} %get-tuple-element.90), channel_id=1, source_target_pairs={{0,1},{1,2},{2,3},{3,4},{4,5},{5,6},{6,7},{8,9},{9,10},{10,11},{11... | collective-permute-start | bytes 1736 | tf_op jit(solution)/shard_map/ppermute | solution.py:20
  164.0 7.5 %collective-permute-start.14 = (f32[8,1,128]{2,0,1:T(8,128)S(1)}, f32[8,1,128]{2,0,1:T(8,128)S(1)}, u32[]{:S(2)}, u32[]{:S(2)}) collective-permute-start(f32[8,1,128]{2,0,1:T(8,128)S(1)} %get-tuple-element.108), channel_id=1, source_target_pairs={{8,0},{16,8},{24,16},{32,24},{40,32},{48,40},{56,48},{64,56},{72,6... | collective-permute-start | bytes 12296 | tf_op jit(solution)/shard_map/ppermute | solution.py:21
  165.9 7.6 %collective-permute-start.15 = (f32[8,1,128]{2,0,1:T(8,128)S(1)}, f32[8,1,128]{2,0,1:T(8,128)S(1)}, u32[]{:S(2)}, u32[]{:S(2)}) collective-permute-start(f32[8,1,128]{2,0,1:T(8,128)S(1)} %get-tuple-element.107), channel_id=1, source_target_pairs={{0,8},{8,16},{16,24},{24,32},{32,40},{40,48},{48,56},{56,64},{64,7... | collective-permute-start | bytes 12296 | tf_op jit(solution)/shard_map/ppermute | solution.py:20
  174.3 14.3 %collective-permute-start.17 = (f32[8,18,1]{2,0,1:T(8,128)}, f32[8,18,1]{2,0,1:T(8,128)}, u32[]{:S(2)}, u32[]{:S(2)}) collective-permute-start(f32[8,18,1]{2,0,1:T(8,128)} %get-tuple-element.88), channel_id=1, source_target_pairs={{0,1},{1,2},{2,3},{3,4},{4,5},{5,6},{6,7},{8,9},{9,10},{10,11},{11... | collective-permute-start | bytes 1736 | tf_op jit(solution)/shard_map/ppermute | solution.py:20
  178.7 9.9 %collective-permute-start.16 = (f32[8,18,1]{2,0,1:T(8,128)}, f32[8,18,1]{2,0,1:T(8,128)}, u32[]{:S(2)}, u32[]{:S(2)}) collective-permute-start(f32[8,18,1]{2,0,1:T(8,128)} %get-tuple-element.87), channel_id=1, source_target_pairs={{1,0},{2,1},{3,2},{4,3},{5,4},{6,5},{7,6},{9,8},{10,9},{11,10},{12... | collective-permute-start | bytes 1736 | tf_op jit(solution)/shard_map/ppermute | solution.py:21
  197.1 7.6 %collective-permute-start.18 = (f32[8,1,64]{2,0,1:T(8,128)S(1)}, f32[8,1,64]{2,0,1:T(8,128)S(1)}, u32[]{:S(2)}, u32[]{:S(2)}) collective-permute-start(f32[8,1,64]{2,0,1:T(8,128)S(1)} %get-tuple-element.126), channel_id=1, source_target_pairs={{8,0},{16,8},{24,16},{32,24},{40,32},{48,40},{56,48},{64,56},{72,6... | collective-permute-start | bytes 6152 | tf_op jit(solution)/shard_map/ppermute | solution.py:21
  199.9 7.6 %collective-permute-start.19 = (f32[8,1,64]{2,0,1:T(8,128)S(1)}, f32[8,1,64]{2,0,1:T(8,128)S(1)}, u32[]{:S(2)}, u32[]{:S(2)}) collective-permute-start(f32[8,1,64]{2,0,1:T(8,128)S(1)} %get-tuple-element.125), channel_id=1, source_target_pairs={{0,8},{8,16},{16,24},{24,32},{32,40},{40,48},{48,56},{56,64},{64,7... | collective-permute-start | bytes 6152 | tf_op jit(solution)/shard_map/ppermute | solution.py:20
  215.1 6.2 %collective-permute-start.22 = (f32[8,1,64]{2,0,1:T(8,128)S(1)}, f32[8,1,64]{2,0,1:T(8,128)S(1)}, u32[]{:S(2)}, u32[]{:S(2)}) collective-permute-start(f32[8,1,64]{2,0,1:T(8,128)S(1)} %get-tuple-element.124), channel_id=1, source_target_pairs={{8,0},{16,8},{24,16},{32,24},{40,32},{48,40},{56,48},{64,56},{72,6... | collective-permute-start | bytes 6152 | tf_op jit(solution)/shard_map/ppermute | solution.py:21
  217.1 7.6 %collective-permute-start.23 = (f32[8,1,64]{2,0,1:T(8,128)S(1)}, f32[8,1,64]{2,0,1:T(8,128)S(1)}, u32[]{:S(2)}, u32[]{:S(2)}) collective-permute-start(f32[8,1,64]{2,0,1:T(8,128)S(1)} %get-tuple-element.123), channel_id=1, source_target_pairs={{0,8},{8,16},{16,24},{24,32},{32,40},{40,48},{48,56},{56,64},{64,7... | collective-permute-start | bytes 6152 | tf_op jit(solution)/shard_map/ppermute | solution.py:20
  233.6 5.9 %collective-permute-start.26 = (f32[8,1,32]{2,0,1:T(8,128)S(1)}, f32[8,1,32]{2,0,1:T(8,128)S(1)}, u32[]{:S(2)}, u32[]{:S(2)}) collective-permute-start(f32[8,1,32]{2,0,1:T(8,128)S(1)} %get-tuple-element.162), channel_id=1, source_target_pairs={{8,0},{16,8},{24,16},{32,24},{40,32},{48,40},{56,48},{64,56},{72,6... | collective-permute-start | bytes 3080 | tf_op jit(solution)/shard_map/ppermute | solution.py:21
  235.5 7.6 %collective-permute-start.27 = (f32[8,1,32]{2,0,1:T(8,128)S(1)}, f32[8,1,32]{2,0,1:T(8,128)S(1)}, u32[]{:S(2)}, u32[]{:S(2)}) collective-permute-start(f32[8,1,32]{2,0,1:T(8,128)S(1)} %get-tuple-element.161), channel_id=1, source_target_pairs={{0,8},{8,16},{16,24},{24,32},{32,40},{40,48},{48,56},{56,64},{64,7... | collective-permute-start | bytes 3080 | tf_op jit(solution)/shard_map/ppermute | solution.py:20
  250.5 6.1 %collective-permute-start.30 = (f32[8,1,32]{2,0,1:T(8,128)S(1)}, f32[8,1,32]{2,0,1:T(8,128)S(1)}, u32[]{:S(2)}, u32[]{:S(2)}) collective-permute-start(f32[8,1,32]{2,0,1:T(8,128)S(1)} %get-tuple-element.160), channel_id=1, source_target_pairs={{8,0},{16,8},{24,16},{32,24},{40,32},{48,40},{56,48},{64,56},{72,6... | collective-permute-start | bytes 3080 | tf_op jit(solution)/shard_map/ppermute | solution.py:21
  252.5 7.6 %collective-permute-start.31 = (f32[8,1,32]{2,0,1:T(8,128)S(1)}, f32[8,1,32]{2,0,1:T(8,128)S(1)}, u32[]{:S(2)}, u32[]{:S(2)}) collective-permute-start(f32[8,1,32]{2,0,1:T(8,128)S(1)} %get-tuple-element.159), channel_id=1, source_target_pairs={{0,8},{8,16},{16,24},{24,32},{32,40},{40,48},{48,56},{56,64},{64,7... | collective-permute-start | bytes 3080 | tf_op jit(solution)/shard_map/ppermute | solution.py:20
  267.8 5.9 %collective-permute-start.34 = (f32[8,1,16]{2,0,1:T(8,128)S(1)}, f32[8,1,16]{2,0,1:T(8,128)S(1)}, u32[]{:S(2)}, u32[]{:S(2)}) collective-permute-start(f32[8,1,16]{2,0,1:T(8,128)S(1)} %get-tuple-element.176), channel_id=1, source_target_pairs={{8,0},{16,8},{24,16},{32,24},{40,32},{48,40},{56,48},{64,56},{72,6... | collective-permute-start | bytes 1544 | tf_op jit(solution)/shard_map/ppermute | solution.py:21
  269.8 7.6 %collective-permute-start.35 = (f32[8,1,16]{2,0,1:T(8,128)S(1)}, f32[8,1,16]{2,0,1:T(8,128)S(1)}, u32[]{:S(2)}, u32[]{:S(2)}) collective-permute-start(f32[8,1,16]{2,0,1:T(8,128)S(1)} %get-tuple-element.175), channel_id=1, source_target_pairs={{0,8},{8,16},{16,24},{24,32},{32,40},{40,48},{48,56},{56,64},{64,7... | collective-permute-start | bytes 1544 | tf_op jit(solution)/shard_map/ppermute | solution.py:20
  284.6 6.1 %collective-permute-start.38 = (f32[8,1,16]{2,0,1:T(8,128)S(1)}, f32[8,1,16]{2,0,1:T(8,128)S(1)}, u32[]{:S(2)}, u32[]{:S(2)}) collective-permute-start(f32[8,1,16]{2,0,1:T(8,128)S(1)} %get-tuple-element.174), channel_id=1, source_target_pairs={{8,0},{16,8},{24,16},{32,24},{40,32},{48,40},{56,48},{64,56},{72,6... | collective-permute-start | bytes 1544 | tf_op jit(solution)/shard_map/ppermute | solution.py:21
  286.5 7.6 %collective-permute-start.39 = (f32[8,1,16]{2,0,1:T(8,128)S(1)}, f32[8,1,16]{2,0,1:T(8,128)S(1)}, u32[]{:S(2)}, u32[]{:S(2)}) collective-permute-start(f32[8,1,16]{2,0,1:T(8,128)S(1)} %get-tuple-element.173), channel_id=1, source_target_pairs={{0,8},{8,16},{16,24},{24,32},{32,40},{40,48},{48,56},{56,64},{64,7... | collective-permute-start | bytes 1544 | tf_op jit(solution)/shard_map/ppermute | solution.py:20
  303.7 7.6 %collective-permute-start.43 = (f32[8,1,8]{2,0,1:T(8,128)S(1)}, f32[8,1,8]{2,0,1:T(8,128)S(1)}, u32[]{:S(2)}, u32[]{:S(2)}) collective-permute-start(f32[8,1,8]{2,0,1:T(8,128)S(1)} %get-tuple-element.5), channel_id=1, source_target_pairs={{0,8},{8,16},{16,24},{24,32},{32,40},{40,48},{48,56},{56,64},{64,7... | collective-permute-start | bytes 776 | tf_op jit(solution)/shard_map/ppermute | solution.py:20
  320.4 7.6 %collective-permute-start.47 = (f32[8,1,8]{2,0,1:T(8,128)S(1)}, f32[8,1,8]{2,0,1:T(8,128)S(1)}, u32[]{:S(2)}, u32[]{:S(2)}) collective-permute-start(f32[8,1,8]{2,0,1:T(8,128)S(1)} %fusion.322), channel_id=1, source_target_pairs={{0,8},{8,16},{16,24},{24,32},{32,40},{40,48},{48,56},{56,64},{64,7... | collective-permute-start | bytes 776 | tf_op jit(solution)/shard_map/ppermute | solution.py:20
  337.0 7.6 %collective-permute-start.51 = (f32[8,1,8]{2,0,1:T(8,128)S(1)}, f32[8,1,8]{2,0,1:T(8,128)S(1)}, u32[]{:S(2)}, u32[]{:S(2)}) collective-permute-start(f32[8,1,8]{2,0,1:T(8,128)S(1)} %fusion.331), channel_id=1, source_target_pairs={{0,8},{8,16},{16,24},{24,32},{32,40},{40,48},{48,56},{56,64},{64,7... | collective-permute-start | bytes 776 | tf_op jit(solution)/shard_map/ppermute | solution.py:20
  353.8 7.6 %collective-permute-start.55 = (f32[8,1,16]{2,0,1:T(8,128)S(1)}, f32[8,1,16]{2,0,1:T(8,128)S(1)}, u32[]{:S(2)}, u32[]{:S(2)}) collective-permute-start(f32[8,1,16]{2,0,1:T(8,128)S(1)} %get-tuple-element.171), channel_id=1, source_target_pairs={{0,8},{8,16},{16,24},{24,32},{32,40},{40,48},{48,56},{56,64},{64,7... | collective-permute-start | bytes 1544 | tf_op jit(solution)/shard_map/ppermute | solution.py:20
  368.6 5.9 %collective-permute-start.58 = (f32[8,1,16]{2,0,1:T(8,128)S(1)}, f32[8,1,16]{2,0,1:T(8,128)S(1)}, u32[]{:S(2)}, u32[]{:S(2)}) collective-permute-start(f32[8,1,16]{2,0,1:T(8,128)S(1)} %get-tuple-element.170), channel_id=1, source_target_pairs={{8,0},{16,8},{24,16},{32,24},{40,32},{48,40},{56,48},{64,56},{72,6... | collective-permute-start | bytes 1544 | tf_op jit(solution)/shard_map/ppermute | solution.py:21
  370.5 7.6 %collective-permute-start.59 = (f32[8,1,16]{2,0,1:T(8,128)S(1)}, f32[8,1,16]{2,0,1:T(8,128)S(1)}, u32[]{:S(2)}, u32[]{:S(2)}) collective-permute-start(f32[8,1,16]{2,0,1:T(8,128)S(1)} %get-tuple-element.169), channel_id=1, source_target_pairs={{0,8},{8,16},{16,24},{24,32},{32,40},{40,48},{48,56},{56,64},{64,7... | collective-permute-start | bytes 1544 | tf_op jit(solution)/shard_map/ppermute | solution.py:20
  387.4 7.6 %collective-permute-start.63 = (f32[8,1,32]{2,0,1:T(8,128)S(1)}, f32[8,1,32]{2,0,1:T(8,128)S(1)}, u32[]{:S(2)}, u32[]{:S(2)}) collective-permute-start(f32[8,1,32]{2,0,1:T(8,128)S(1)} %get-tuple-element.137), channel_id=1, source_target_pairs={{0,8},{8,16},{16,24},{24,32},{32,40},{40,48},{48,56},{56,64},{64,7... | collective-permute-start | bytes 3080 | tf_op jit(solution)/shard_map/ppermute | solution.py:20
  402.2 5.9 %collective-permute-start.66 = (f32[8,1,32]{2,0,1:T(8,128)S(1)}, f32[8,1,32]{2,0,1:T(8,128)S(1)}, u32[]{:S(2)}, u32[]{:S(2)}) collective-permute-start(f32[8,1,32]{2,0,1:T(8,128)S(1)} %get-tuple-element.136), channel_id=1, source_target_pairs={{8,0},{16,8},{24,16},{32,24},{40,32},{48,40},{56,48},{64,56},{72,6... | collective-permute-start | bytes 3080 | tf_op jit(solution)/shard_map/ppermute | solution.py:21
  404.1 7.6 %collective-permute-start.67 = (f32[8,1,32]{2,0,1:T(8,128)S(1)}, f32[8,1,32]{2,0,1:T(8,128)S(1)}, u32[]{:S(2)}, u32[]{:S(2)}) collective-permute-start(f32[8,1,32]{2,0,1:T(8,128)S(1)} %get-tuple-element.135), channel_id=1, source_target_pairs={{0,8},{8,16},{16,24},{24,32},{32,40},{40,48},{48,56},{56,64},{64,7... | collective-permute-start | bytes 3080 | tf_op jit(solution)/shard_map/ppermute | solution.py:20
  419.3 5.9 %collective-permute-start.70 = (f32[8,1,64]{2,0,1:T(8,128)S(1)}, f32[8,1,64]{2,0,1:T(8,128)S(1)}, u32[]{:S(2)}, u32[]{:S(2)}) collective-permute-start(f32[8,1,64]{2,0,1:T(8,128)S(1)} %get-tuple-element.122), channel_id=1, source_target_pairs={{8,0},{16,8},{24,16},{32,24},{40,32},{48,40},{56,48},{64,56},{72,6... | collective-permute-start | bytes 6152 | tf_op jit(solution)/shard_map/ppermute | solution.py:21
  421.2 7.6 %collective-permute-start.71 = (f32[8,1,64]{2,0,1:T(8,128)S(1)}, f32[8,1,64]{2,0,1:T(8,128)S(1)}, u32[]{:S(2)}, u32[]{:S(2)}) collective-permute-start(f32[8,1,64]{2,0,1:T(8,128)S(1)} %get-tuple-element.121), channel_id=1, source_target_pairs={{0,8},{8,16},{16,24},{24,32},{32,40},{40,48},{48,56},{56,64},{64,7... | collective-permute-start | bytes 6152 | tf_op jit(solution)/shard_map/ppermute | solution.py:20
  436.2 5.9 %collective-permute-start.74 = (f32[8,1,64]{2,0,1:T(8,128)S(1)}, f32[8,1,64]{2,0,1:T(8,128)S(1)}, u32[]{:S(2)}, u32[]{:S(2)}) collective-permute-start(f32[8,1,64]{2,0,1:T(8,128)S(1)} %get-tuple-element.120), channel_id=1, source_target_pairs={{8,0},{16,8},{24,16},{32,24},{40,32},{48,40},{56,48},{64,56},{72,6... | collective-permute-start | bytes 6152 | tf_op jit(solution)/shard_map/ppermute | solution.py:21
  438.1 7.6 %collective-permute-start.75 = (f32[8,1,64]{2,0,1:T(8,128)S(1)}, f32[8,1,64]{2,0,1:T(8,128)S(1)}, u32[]{:S(2)}, u32[]{:S(2)}) collective-permute-start(f32[8,1,64]{2,0,1:T(8,128)S(1)} %get-tuple-element.119), channel_id=1, source_target_pairs={{0,8},{8,16},{16,24},{24,32},{32,40},{40,48},{48,56},{56,64},{64,7... | collective-permute-start | bytes 6152 | tf_op jit(solution)/shard_map/ppermute | solution.py:20
  453.6 5.9 %collective-permute-start.78 = (f32[8,1,128]{2,0,1:T(8,128)S(1)}, f32[8,1,128]{2,0,1:T(8,128)S(1)}, u32[]{:S(2)}, u32[]{:S(2)}) collective-permute-start(f32[8,1,128]{2,0,1:T(8,128)S(1)} %get-tuple-element.94), channel_id=1, source_target_pairs={{8,0},{16,8},{24,16},{32,24},{40,32},{48,40},{56,48},{64,56},{72,6... | collective-permute-start | bytes 12296 | tf_op jit(solution)/shard_map/ppermute | solution.py:21
  455.5 7.6 %collective-permute-start.79 = (f32[8,1,128]{2,0,1:T(8,128)S(1)}, f32[8,1,128]{2,0,1:T(8,128)S(1)}, u32[]{:S(2)}, u32[]{:S(2)}) collective-permute-start(f32[8,1,128]{2,0,1:T(8,128)S(1)} %get-tuple-element.93), channel_id=1, source_target_pairs={{0,8},{8,16},{16,24},{24,32},{32,40},{40,48},{48,56},{56,64},{64,7... | collective-permute-start | bytes 12296 | tf_op jit(solution)/shard_map/ppermute | solution.py:20
  470.6 5.9 %collective-permute-start.82 = (f32[8,1,128]{2,0,1:T(8,128)S(1)}, f32[8,1,128]{2,0,1:T(8,128)S(1)}, u32[]{:S(2)}, u32[]{:S(2)}) collective-permute-start(f32[8,1,128]{2,0,1:T(8,128)S(1)} %get-tuple-element.92), channel_id=1, source_target_pairs={{8,0},{16,8},{24,16},{32,24},{40,32},{48,40},{56,48},{64,56},{72,6... | collective-permute-start | bytes 12296 | tf_op jit(solution)/shard_map/ppermute | solution.py:21
  472.6 7.6 %collective-permute-start.83 = (f32[8,1,128]{2,0,1:T(8,128)S(1)}, f32[8,1,128]{2,0,1:T(8,128)S(1)}, u32[]{:S(2)}, u32[]{:S(2)}) collective-permute-start(f32[8,1,128]{2,0,1:T(8,128)S(1)} %get-tuple-element.91), channel_id=1, source_target_pairs={{0,8},{8,16},{16,24},{24,32},{32,40},{40,48},{48,56},{56,64},{64,7... | collective-permute-start | bytes 12296 | tf_op jit(solution)/shard_map/ppermute | solution.py:20
  488.8 5.9 %collective-permute-start.86 = (f32[8,1,256]{2,0,1:T(8,128)S(1)}, f32[8,1,256]{2,0,1:T(8,128)S(1)}, u32[]{:S(2)}, u32[]{:S(2)}) collective-permute-start(f32[8,1,256]{2,0,1:T(8,128)S(1)} %get-tuple-element.60), channel_id=1, source_target_pairs={{8,0},{16,8},{24,16},{32,24},{40,32},{48,40},{56,48},{64,56},{72,6... | collective-permute-start | bytes 24584 | tf_op jit(solution)/shard_map/ppermute | solution.py:21
  490.7 7.7 %collective-permute-start.87 = (f32[8,1,256]{2,0,1:T(8,128)S(1)}, f32[8,1,256]{2,0,1:T(8,128)S(1)}, u32[]{:S(2)}, u32[]{:S(2)}) collective-permute-start(f32[8,1,256]{2,0,1:T(8,128)S(1)} %get-tuple-element.59), channel_id=1, source_target_pairs={{0,8},{8,16},{16,24},{24,32},{32,40},{40,48},{48,56},{56,64},{64,7... | collective-permute-start | bytes 24584 | tf_op jit(solution)/shard_map/ppermute | solution.py:20
  506.8 5.9 %collective-permute-start.90 = (f32[8,1,256]{2,0,1:T(8,128)S(1)}, f32[8,1,256]{2,0,1:T(8,128)S(1)}, u32[]{:S(2)}, u32[]{:S(2)}) collective-permute-start(f32[8,1,256]{2,0,1:T(8,128)S(1)} %get-tuple-element.58), channel_id=1, source_target_pairs={{8,0},{16,8},{24,16},{32,24},{40,32},{48,40},{56,48},{64,56},{72,6... | collective-permute-start | bytes 24584 | tf_op jit(solution)/shard_map/ppermute | solution.py:21
  508.7 7.7 %collective-permute-start.91 = (f32[8,1,256]{2,0,1:T(8,128)S(1)}, f32[8,1,256]{2,0,1:T(8,128)S(1)}, u32[]{:S(2)}, u32[]{:S(2)}) collective-permute-start(f32[8,1,256]{2,0,1:T(8,128)S(1)} %get-tuple-element.57), channel_id=1, source_target_pairs={{0,8},{8,16},{16,24},{24,32},{32,40},{40,48},{48,56},{56,64},{64,7... | collective-permute-start | bytes 24584 | tf_op jit(solution)/shard_map/ppermute | solution.py:20
  (66 other events, 1223.5 us)
where the time goes:
time: 534 us; the launch traced here: 526 us
  starting transfers between devices  252 us (47%)
  waiting for transfers between devices  131 us (25%)
  local copies, waits for them, and re-layouts  125 us (23%)
  other arithmetic  15.4 us (3%)
    ppermute x46, starting transfers between devices, padded_2(): before = lax.ppermute(last, axis, up)  164 us
    ppermute x46, starting transfers between devices, padded_2(): after = lax.ppermute(initial, axis, down)  82.7 us
    ppermute x46, waiting for transfers between devices, padded_2(): before = lax.ppermute(last, axis, up)  80.9 us
    ppermute x46, waiting for transfers between devices, padded_2(): after = lax.ppermute(initial, axis, down)  50.1 us
    unnamed x101, local copies, waits for them, and re-layouts  45.9 us
    slice x15, local copies, waits for them, and re-layouts, restrict(): blocks[:, :, 0, :, 1]  28.9 us
    slice x10, local copies, waits for them, and re-layouts, coarsen(): coarse_x = (face_x[:, 1::2, 0::2] + face_x[:, 1::2, 1::2]) * 0.25  11.6 us
    slice x10, local copies, waits for them, and re-layouts, coarsen(): coarse_y = (face_y[:, 0::2, 1::2] + face_y[:, 1::2, 1::2]) * 0.25  11.1 us
  transfers between devices with their start and end apart: 94, of which 44 were waited for; matrix products, arithmetic and copies ran while one was open for 15% of the time, Pallas kernels for 0%

commit v1 on v0

v1 whole, which is shorter than its diff:
```python
import jax
import jax.numpy as jnp
from jax import lax
from jax.experimental import pallas as pl
from jax.experimental.pallas import tpu as pltpu
from jax.sharding import PartitionSpec as P

DAMPING = 0.8
F32 = jnp.float32
MESH = pl.DeviceIdType.MESH
NZ, R0, C0 = 8, 32, 256
OWN = (4, 16, 8, 4, 12, 6)
ROWS = (40, 48, 24, 12, 26, 12)
LANES = (384, 256, 128, 128, 128, 128)
REACH = 6


def lanes_of(shape):
    return lax.broadcasted_iota(jnp.int32, shape, len(shape) - 1)


def left(values):
    return pltpu.roll(values, values.shape[-1] - 1, values.ndim - 1)


def right(values):
    return pltpu.roll(values, 1, values.ndim - 1)


def above(values):
    return pltpu.roll(values, values.shape[-2] - 1, values.ndim - 2)


def below(values):
    return pltpu.roll(values, 1, values.ndim - 2)


def take(values, index):
    rows = values.size // 128
    flat = jnp.take_along_axis(values.reshape(rows, 128), jnp.broadcast_to(index, (rows, 128)), axis=1)
    return flat.reshape(values.shape)


def squeeze(first, second, odd=False):
    lane = lanes_of((1, 128))
    index = (2 * lane + (1 if odd else 0)) & 127
    one = take(first, index)
    if second is None:
        return one
    return jnp.where(lanes_of(first.shape) < 64, one, take(second, index))


def pair(values):
    return values + pltpu.roll(values, 127, values.ndim - 1)


def squeeze_wide(values, odd=False, sums=True):
    parts = [values[..., 128 * j : 128 * j + 128] for j in range(values.shape[-1] // 128)]
    if sums:
        parts = [pair(p) for p in parts]
    return squeeze(parts[0], parts[1] if len(parts) > 1 else None, odd)


def stretch_index(kind):
    lane = lanes_of((1, 128))
    half = lane // 2
    if kind == "low":
        return half
    if kind == "high":
        return half + 64
    split = 64 if kind == "ends" else 96
    return half + jnp.where(lane >= split, 64, 0)


def chunks(lo, hi, step, body):
    whole = (hi - lo) // step
    if whole > 1:
        lax.fori_loop(0, whole, lambda n, c: (body(lo + n * step, step), c)[1], 0)
    elif whole == 1:
        body(lo, step)
    if (hi - lo) % step:
        body(lo + whole * step, (hi - lo) % step)


class Level:
    def __init__(self, level, a, d, rd, va, vb):
        self.level, self.a, self.d, self.rd, self.va, self.vb = level, a, d, rd, va, vb
        self.own = OWN[level]
        self.step = (4, 4, 8, 8, 8, 8)[level]

    def rows(self, ref, i, k):
        return ref[pl.ds(i + self.own, k)]

    def field(self, f, i, k):
        return self.a[f, pl.ds(i + self.own, k)]

    def diagonal(self, lo, hi):
        def body(i, k):
            kappa = self.field(1, i, k)
            fx, fxl, fy, fz = self.field(2, i, k), self.field(2, i - 1, k), self.field(3, i, k), self.field(4, i, k)
            d = kappa + fx + fxl + fy + right(fy) + fz + below(fz)
            self.d[pl.ds(i + self.own, k)] = d
            self.rd[pl.ds(i + self.own, k)] = jnp.where(kappa > 0, DAMPING / d, 0.0)

        chunks(lo, hi, self.step, body)

    def beside(self, v, i, k):
        c = self.rows(v, i, k)
        fx, fxl, fy, fz = self.field(2, i, k), self.field(2, i - 1, k), self.field(3, i, k), self.field(4, i, k)
        total = fx * self.rows(v, i + 1, k) + fxl * self.rows(v, i - 1, k)
        total = total + fy * left(c) + right(fy * c)
        total = total + fz * above(c) + below(fz * c)
        return c, total

    def first(self, lo, hi, out):
        def body(i, k):
            out[pl.ds(i + self.own, k)] = self.rows(self.rd, i, k) * self.field(0, i, k)

        chunks(lo, hi, self.step, body)

    def sweep(self, lo, hi, v, out):
        def body(i, k):
            c, total = self.beside(v, i, k)
            new = (1 - DAMPING) * c + self.rows(self.rd, i, k) * (self.field(0, i, k) + total)
            out[pl.ds(i + self.own, k)] = new

        chunks(lo, hi, self.step, body)

    def restrict_residual(self, lo, hi, v, coarse):
        def body(n, m):
            k = 2 * m
            i = 2 * n
            c, total = self.beside(v, i, k)
            residual = self.field(0, i, k) - self.rows(self.d, i, k) * c + total
            residual = residual[..., : min(residual.shape[-1], 256)]
            residual = residual.reshape(m, 2, *residual.shape[1:])
            coarse.a[0, pl.ds(n + coarse.own, m)] = fit(squeeze_wide(residual[:, 0] + residual[:, 1]) * 0.25, coarse)

        chunks(lo // 2, hi // 2, self.step // 2, body)

    def coarsen(self, lo, hi, coarse, fx_low=None):
        def body(n, m):
            both = [self.field(f, 2 * n, 2 * m)[..., : min(self.a.shape[-1], 256)] for f in (1, 2, 3, 4)]
            both = [b.reshape(m, 2, *b.shape[1:]) for b in both]
            kappa, fx, fy, fz = both
            at = pl.ds(n + coarse.own, m)
            coarse.a[1, at] = fit(squeeze_wide(kappa[:, 0] + kappa[:, 1]) * 0.25, coarse)
            coarse.a[2, at] = fit(squeeze_wide(fx[:, 1]) * 0.25, coarse)
            coarse.a[3, at] = fit(squeeze_wide(fy[:, 0] + fy[:, 1], odd=True, sums=False) * 0.25, coarse)
            coarse.a[4, at] = fit(squeeze_wide(fz[:, 0] + fz[:, 1]) * 0.25, coarse)

        chunks(lo, hi, self.step // 2, body)
        if fx_low is not None:
            fx = self.field(2, 2 * fx_low + 1, 1)
            coarse.a[2, pl.ds(fx_low + coarse.own, 1)] = squeeze_wide(fx) * 0.25

    def correct(self, lo, hi, v, coarse, c, out):
        def body(n, m):
            values = c[pl.ds(n + coarse.own, m)]
            if self.level == 0:
                first, second = values[..., :128], values[..., 128:]
                fine = [take(first, stretch_index("low")), take(first, stretch_index("high")), take(second, stretch_index("ends"))]
            elif self.level == 1:
                fine = [take(values, stretch_index("low")), take(values, stretch_index("high"))]
            else:
                fine = [take(values, stretch_index("late"))]
            for j, part in enumerate(fine):
                cols = slice(128 * j, 128 * j + 128)
                at = pl.ds(2 * n + self.own, 2 * m)
                spread = jnp.broadcast_to(part[:, None], (m, 2, NZ, 128)).reshape(2 * m, NZ, 128)
                out[at, :, cols] = v[at, :, cols] + spread

        chunks(lo // 2, hi // 2, max(self.step // 2, 1), body)


def fit(values, coarse):
    if coarse.level == 1:
        return jnp.concatenate([values, jnp.zeros_like(values)], axis=-1)
    return values


def kernel(gx, gy, source, kappa_sq, face_x, face_y, face_z, field, *refs):
    refs = list(refs)

    def get(n):
        out = refs[:n]
        del refs[:n]
        return out

    raw_s, raw_c, wide, out_v = get(4)
    levels = []
    for n in range(6):
        levels.append(Level(n, *get(5)))
    send0, recv0, send1, recv1, sendr, recvr = get(6)
    send4, recv4, wide4, recv4x = get(4)
    sendv, recvv, widev, recvvx, recv3x = get(5)
    load_sem, store_sem, ssem, rsem = get(4)
    l0, l1, l2, l3, l4, l5 = levels

    mx, my = lax.axis_index("gx"), lax.axis_index("gy")

    loads = []
    for h in range(2):
        cols = pl.ds(128 * h, 128)
        loads.append(pltpu.make_async_copy(source.at[:, :, cols], raw_s.at[h], load_sem.at[h, 0]))
        for f, ref in enumerate((kappa_sq, face_x, face_y, face_z)):
            loads.append(pltpu.make_async_copy(ref.at[:, :, cols], raw_c.at[h, f], load_sem.at[h, f + 1]))
    for copy in loads:
        copy.start()

    transfers = {}

    def plan(name, src, dst, dx, dy):
        transfers[name] = (src, dst, dx, dy, len(transfers))

    def there(dx):
        if dx == 0:
            return None
        return mx + dx < gx if dx > 0 else mx + dx >= 0

    def when(cond, action):
        if cond is None:
            action()
        else:
            pl.when(cond)(action)

    def copy_of(name):
        src, dst, dx, dy, n = transfers[name]
        ids = (mx + dx, lax.rem(my + dy + gy, gy))
        return pltpu.make_async_remote_copy(
            src_ref=src, dst_ref=dst, send_sem=ssem.at[n], recv_sem=rsem.at[n], device_id=ids, device_id_type=MESH
        )

    def grouped(names, action, sign):
        by = {}
        for name in names:
            by.setdefault(transfers[name][2], []).append(name)
        for dx, group in by.items():

            def go(group=group):
                for name in group:
                    action(copy_of(name))

            when(there(sign * dx), go)

    def send(names):
        grouped(names, lambda c: c.start(), 1)

    def arrive(names):
        grouped(names, lambda c: c.wait_recv(), -1)

    for d in (1, -1):
        a0, a1 = l0.a, l1.a
        s0, t0 = (33, 1) if d == 1 else (4, 36)
        cols = pl.ds(0, C0)
        plan(("x0", d), a0.at[:, pl.ds(s0, 3), :, cols], a0.at[:, pl.ds(t0, 3), :, cols], d, 0)
        if d == 1:
            plan(("x0f", d), a0.at[2, pl.ds(32, 1), :, cols], a0.at[2, pl.ds(0, 1), :, cols], d, 0)
        cols = pl.ds(0, 128)
        s1, t1, n1 = (17, 1, 15) if d == 1 else (16, 32, 14)
        plan(("x1", d), a1.at[pl.ds(1, 4), pl.ds(s1, n1), :, cols], a1.at[pl.ds(1, 4), pl.ds(t1, n1), :, cols], d, 0)
        s1, t1 = (18, 2) if d == 1 else (16, 32)
        plan(("xr", d), a1.at[0, pl.ds(s1, 14), :, cols], a1.at[0, pl.ds(t1, 14), :, cols], d, 0)
    for dy in (1, -1):
        e = (dy + 1) // 2
        for dx in (-1, 0, 1):
            plan(("y0", dx, dy), send0.at[e], recv0.at[e, dx + 1], dx, dy)
            plan(("y1", dx, dy), send1.at[e], recv1.at[e, dx + 1], dx, dy)
            plan(("yr", dx, dy), sendr.at[e], recvr.at[e, dx + 1], dx, dy)
        plan(("y4", dy), send4, recv4.at[e], 0, dy)
        plan(("yv", dy), sendv, recvv.at[e], 0, dy)
    far = [s * k for k in range(1, REACH + 1) for s in (1, -1)]
    for n, dx in enumerate(far):
        plan(("x4", dx), wide4, recv4x.at[n], dx, 0)
        plan(("xv", dx), widev.at[0], recvvx.at[n], dx, 0)
    for n, dx in enumerate((1, -1)):
        plan(("x3", dx), widev.at[pl.ds(1, 4)], recv3x.at[n], dx, 0)

    def zero(ref, *index):
        ref[index] = jnp.zeros(ref[index].shape, F32)

    @pl.when(mx == 0)
    def _():
        l0.a[:, 0:4] = jnp.zeros((5, 4, NZ, 384), F32)
        l1.a[:, 0:16] = jnp.zeros((5, 16, NZ, 256), F32)
        recv3x[0] = jnp.zeros((4, NZ, 128), F32)

    @pl.when(mx == gx - 1)
    def _():
        l0.a[:, 36:40] = jnp.zeros((5, 4, NZ, 384), F32)
        l1.a[:, 32:48] = jnp.zeros((5, 16, NZ, 256), F32)
        recv3x[1] = jnp.zeros((4, NZ, 128), F32)

    for n, dx in enumerate(far):

        @pl.when(jnp.logical_not(there(-dx)))
        def _(n=n):
            recv4x[n] = jnp.zeros((4, NZ, 128), F32)
            recvvx[n] = jnp.zeros((NZ, 128), F32)

    barrier = pltpu.get_barrier_semaphore()
    partners = [(0, 1), (0, -1)] + [(dx, 0) for dx in far] + [(dx, dy) for dx in (1, -1) for dy in (1, -1)]
    count = 0
    for dx in [0] + far:
        group = [p for p in partners if p[0] == dx]

        def greet(group=group):
            for px, py in group:
                ids = (mx + px, lax.rem(my + py + gy, gy))
                pl.semaphore_signal(barrier, inc=1, device_id=ids, device_id_type=MESH)

        when(there(dx), greet)
        count = count + (len(group) if dx == 0 else jnp.where(there(dx), len(group), 0))

    for copy in loads:
        copy.wait()

    def widen(h, c):
        for f in range(4):
            wide[h, f] = raw_c[h, f].reshape(256, 128).astype(F32)
        top = pl.ds(224, 32)
        wide[h, 0, top] = wide[h, 0, top] + wide[h, 3, top]
        wide[h, 3, top] = jnp.zeros((32, 128), F32)
        return c

    for h in range(2):
        widen(h, 0)

    def turn(i):
        for h in range(2):
            cols = slice(128 * h, 128 * h + 128)
            l0.a[0, 4 + i, :, cols] = raw_s.at[h].reshape(256, 128)[pl.ds(i, NZ, stride=32), :]
            for f in range(4):
                l0.a[1 + f, 4 + i, :, cols] = wide.at[h, f][pl.ds(i, NZ, stride=32), :]

    edge = [0, 1, 2, 28, 29, 30, 31]
    for i in edge:
        turn(i)
    pl.semaphore_wait(barrier, count)
    send([("x0", 1), ("x0f", 1), ("x0", -1)])
    for i in range(3, 28):
        turn(i)

    def pack(a, fields, own, count, width, last, dst):
        per = 128 // width
        lane = lanes_of((NZ, 128))
        for e in range(2):
            at = pl.ds(last, 128) if e == 1 else pl.ds(0, 128)
            for g in range(count // per):
                total = None
                for j in range(per):
                    row = a[fields, own + g * per + j, :, at]
                    shift = (width * j + (width if e == 1 else 0)) % 128
                    row = pltpu.roll(row, shift, row.ndim - 1) if shift else row
                    total = row if total is None else jnp.where(lane // width == j, row, total)
                dst[e, g] = total

    has_left, has_right = my > 0, my < gy - 1

    def unpack(src, a, fields, own, count, width, last, rows):
        per = 128 // width
        lane = lanes_of((NZ, 128))
        for i in rows:
            dx = -1 if i < 0 else (1 if i >= count else 0)
            j = i - dx * count
            keep_r, keep_l = has_right, has_left
            if dx:
                keep_r, keep_l = keep_r & there(dx), keep_l & there(dx)
            from_r, from_l = src[0, 1 - dx, j // per], src[1, 1 - dx, j // per]
            shift = (128 - width * (j % per)) % 128
            from_r = pltpu.roll(from_r, shift, from_r.ndim - 1) if shift else from_r
            shift = (shift + 128 - width) % 128
            from_l = pltpu.roll(from_l, shift, from_l.ndim - 1) if shift else from_l
            row = jnp.where((lane < width) & keep_r, from_r, jnp.where((lane >= 128 - width) & keep_l, from_l, 0.0))
            a[fields, own + i, :, pl.ds(last, 128)] = row

    all_fields, coefs = slice(0, 5), slice(1, 5)
    sides = [(dx, dy) for dy in (1, -1) for dx in (0, -1, 1)]
    pack(l0.a, all_fields, 4, 32, 4, 128, send0)
    send([("y0", *p) for p in sides])

    l0.coarsen(0, 16, l1)
    pack(l1.a, coefs, 16, 16, 16, 0, send1)
    send([("x1", 1), ("x1", -1)] + [("y1", *p) for p in sides])
    l1.coarsen(0, 8, l2)
    l2.coarsen(0, 4, l3)
    l3.coarsen(0, 2, l4)
    lane = lanes_of((NZ, 128))
    send4[...] = jnp.where(lane < 64, l4.a[1:5, 12], pltpu.roll(l4.a[1:5, 13], 64, 2))
    send([("y4", 1), ("y4", -1)])

    arrive([("x0", 1), ("x0f", 1), ("x0", -1)] + [("y0", *p) for p in sides])
    unpack(recv0, l0.a, all_fields, 4, 32, 4, 256, range(-4, 35))
    l0.diagonal(-3, 35)
    l0.first(-3, 35, l0.va)
    l0.sweep(-2, 34, l0.va, l0.vb)
    l0.restrict_residual(0, 32, l0.vb, l1)
    send([("xr", 1), ("xr", -1)])
    pack(l1.a, 0, 16, 16, 16, 0, sendr)
    send([("yr", *p) for p in sides])

    def join(own, from_r, from_l, size):
        shape = own.shape
        at = lanes_of(shape) & 63
        keep_r = (at >= size) & (at < 48) & has_right
        keep_l = (at >= 48) & has_left
        from_r = pltpu.roll(from_r, size, len(shape) - 1)
        from_l = pltpu.roll(from_l, 128 - size, len(shape) - 1)
        return jnp.where(at < size, own, jnp.where(keep_r, from_r, jnp.where(keep_l, from_l, 0.0)))

    arrive([("y4", 1), ("y4", -1)])
    wide4[...] = join(send4[...], recv4[0], recv4[1], 16)
    send([("x4", dx) for dx in far])

    arrive([("x1", 1), ("x1", -1)] + [("y1", *p) for p in sides])
    unpack(recv1, l1.a, coefs, 16, 16, 16, 128, range(-15, 30))
    l1.diagonal(-14, 30)
    l1.coarsen(-7, 15, l2)
    l2.diagonal(-6, 14)
    l2.coarsen(-3, 7, l3, fx_low=-4)
    l3.diagonal(-3, 7)
    l3.coarsen(-1, 2, l4)
    l4.diagonal(0, 2)

    arrive([("xr", 1), ("xr", -1)] + [("yr", *p) for p in sides])
    unpack(recvr, l1.a, 0, 16, 16, 16, 128, range(-14, 30))
    l1.first(-14, 30, l1.va)
    l1.sweep(-13, 29, l1.va, l1.vb)
    l1.restrict_residual(-12, 28, l1.vb, l2)
    l2.first(-6, 14, l2.va)
    l2.sweep(-5, 13, l2.va, l2.vb)
    l2.restrict_residual(-4, 12, l2.vb, l3)
    l3.first(-2, 6, l3.va)
    l3.sweep(-1, 5, l3.va, l3.vb)
    l3.restrict_residual(0, 4, l3.vb, l4)
    l4.first(0, 2, l4.va)

    def two(ref, i):
        return jnp.where(lane < 64, ref[i], pltpu.roll(ref[i + 1], 64, 1))

    sendv[0] = two(l4.va, 12)
    for n in range(2):
        sendv[1 + n] = two(l3.a.at[0], 4 + 2 * n)
        sendv[3 + n] = two(l3.vb, 4 + 2 * n)
    send([("yv", 1), ("yv", -1)])

    def spread_two(both, ref, i):
        ref[i] = both
        ref[i + 1] = pltpu.roll(both, 64, both.ndim - 1)

    def own_and_far(ref, n_field, i_own):
        return

    arrive([("x4", dx) for dx in far])
    for n, dx in list(enumerate(far)) + [(None, 0)]:
        both = wide4[...] if dx == 0 else recv4x[n]
        i = 12 - 2 * dx
        l4.a[1:5, i] = both
        l4.a[1:5, i + 1] = pltpu.roll(both, 64, 2)
    l4.diagonal(-11, 13)
    l4.coarsen(-5, 6, l5, fx_low=-6)
    l5.diagonal(-5, 6)

    arrive([("yv", 1), ("yv", -1)])
    widev[0] = join(sendv[0], recvv[0, 0], recvv[1, 0], 16)
    send([("xv", dx) for dx in far])
    widev[1:5] = join(sendv[1:5], recvv[0, 1:5], recvv[1, 1:5], 32)
    send([("x3", 1), ("x3", -1)])
    arrive([("xv", dx) for dx in far])
    for n, dx in list(enumerate(far)) + [(None, 0)]:
        spread_two(widev[0] if dx == 0 else recvvx[n], l4.va, 12 - 2 * dx)

    def body(i, k):
        l4.a[0, pl.ds(i + 12, k)] = l4.rows(l4.va, i, k) * l4.rows(l4.d, i, k) * (1 / DAMPING)

    chunks(-11, 13, 8, body)
    l4.sweep(-11, 13, l4.va, l4.vb)
    l4.restrict_residual(-10, 12, l4.vb, l5)

    l5.first(-5, 6, l5.va)
    l5.sweep(-4, 5, l5.va, l5.vb)
    l5.sweep(-3, 4, l5.vb, l5.va)
    l5.sweep(-2, 3, l5.va, l5.vb)

    l4.correct(-4, 6, l4.vb, l5, l5.vb, l4.va)
    l4.sweep(-3, 5, l4.va, l4.vb)
    l4.sweep(-2, 4, l4.vb, l4.va)

    arrive([("x3", 1), ("x3", -1)])
    for src, dx in ((widev.at[pl.ds(1, 4)], 0), (recv3x.at[0], 1), (recv3x.at[1], -1)):
        for n in range(2):
            i = 4 - 4 * dx + 2 * n
            spread_two(src[n], l3.a.at[0], i)
            spread_two(src[2 + n], l3.vb, i)
    l3.correct(-4, 8, l3.vb, l4, l4.va, l3.va)
    l3.sweep(-3, 7, l3.va, l3.vb)
    l3.sweep(-2, 6, l3.vb, l3.va)

    l2.correct(-4, 12, l2.vb, l3, l3.va, l2.va)
    l2.sweep(-3, 11, l2.va, l2.vb)
    l2.sweep(-2, 10, l2.vb, l2.va)

    l1.correct(-4, 20, l1.vb, l2, l2.va, l1.va)
    l1.sweep(-2, 18, l1.va, l1.vb)
    l1.sweep(-1, 17, l1.vb, l1.va)

    l0.correct(-2, 34, l0.vb, l1, l1.va, l0.va)
    l0.sweep(-1, 33, l0.va, l0.vb)

    def last(n, c):
        for q in range(2):
            i = 8 * n + 4 * q
            mid, total = l0.beside(l0.vb, i, 4)
            new = (1 - DAMPING) * mid + l0.rows(l0.rd, i, 4) * (l0.field(0, i, 4) + total)
            for j in range(4):
                for h in range(2):
                    out_v.at[h].reshape(256, 128)[pl.ds(i + j, NZ, stride=32), :] = new[j, :, 128 * h : 128 * h + 128]
        return c

    for n in range(4):
        last(n, 0)
        for h in range(2):
            rows, cols = pl.ds(8 * n, 8), pl.ds(128 * h, 128)
            pltpu.make_async_copy(out_v.at[h, :, rows], field.at[:, rows, cols], store_sem.at[n, h]).start()

    grouped(list(transfers), lambda c: c.wait_send(), 1)
    for n in range(4):
        for h in range(2):
            rows, cols = pl.ds(8 * n, 8), pl.ds(128 * h, 128)
            pltpu.make_async_copy(out_v.at[h, :, rows], field.at[:, rows, cols], store_sem.at[n, h]).wait()


def solution(mesh):
    gx, gy = mesh.shape["gx"], mesh.shape["gy"]
    number = 2 + 1 + 2 + 2 + 18 + 4 + 4 * REACH + 2

    def step(*args):
        scratch = [
            pltpu.VMEM((2, NZ, R0, 128), F32),
            pltpu.VMEM((2, 4, NZ, R0, 128), jnp.bfloat16),
            pltpu.VMEM((2, 4, NZ * R0, 128), F32),
            pltpu.VMEM((2, NZ, R0, 128), F32),
        ]
        for rows, cols in zip(ROWS, LANES):
            scratch.append(pltpu.VMEM((5, rows, NZ, cols), F32))
            scratch += [pltpu.VMEM((rows, NZ, cols), F32)] * 4
        scratch += [
            pltpu.VMEM((2, 1, 5, NZ, 128), F32),
            pltpu.VMEM((2, 3, 1, 5, NZ, 128), F32),
            pltpu.VMEM((2, 2, 4, NZ, 128), F32),
            pltpu.VMEM((2, 3, 2, 4, NZ, 128), F32),
            pltpu.VMEM((2, 2, NZ, 128), F32),
            pltpu.VMEM((2, 3, 2, NZ, 128), F32),
            pltpu.VMEM((4, NZ, 128), F32),
            pltpu.VMEM((2, 4, NZ, 128), F32),
            pltpu.VMEM((4, NZ, 128), F32),
            pltpu.VMEM((2 * REACH, 4, NZ, 128), F32),
            pltpu.VMEM((5, NZ, 128), F32),
            pltpu.VMEM((2, 5, NZ, 128), F32),
            pltpu.VMEM((5, NZ, 128), F32),
            pltpu.VMEM((2 * REACH, NZ, 128), F32),
            pltpu.VMEM((2, 4, NZ, 128), F32),
            pltpu.SemaphoreType.DMA((2, 5)),
            pltpu.SemaphoreType.DMA((4, 2)),
            pltpu.SemaphoreType.DMA((number,)),
            pltpu.SemaphoreType.DMA((number,)),
        ]

        def body(*refs):
            kernel(gx, gy, *refs)

        return pl.pallas_call(
            body,
            out_shape=jax.ShapeDtypeStruct((NZ, R0, C0), F32),
            in_specs=[pl.BlockSpec(memory_space=pl.ANY)] * 5,
            out_specs=pl.BlockSpec(memory_space=pl.ANY),
            scratch_shapes=scratch,
            compiler_params=pltpu.CompilerParams(
                collective_id=0, has_side_effects=True, vmem_limit_bytes=40 * 2**20
            ),
        )(*args)

    placed = P(None, "gx", "gy")
    return jax.shard_map(step, mesh=mesh, in_specs=(placed,) * 5, out_specs=placed, check_vma=False)
```

time: 534 us -> 58.7 us (0.11); the launches traced: 526 us -> 58.5 us
  starting transfers between devices: 252 us -> 0 us
  waiting for transfers between devices: 131 us -> 0 us
  local copies, waits for them, and re-layouts: 125 us -> 5.27 us
  Pallas kernels: 0 us -> 53.2 us
  other arithmetic: 15.4 us -> 0 us
    ppermute x94 -> x0, starting transfers between devices: 252 us -> none  [the longest x46 164 us: padded_2(): before = lax.ppermute(last, axis, up)]
    ppermute x94 -> x0, waiting for transfers between devices: 131 us -> none  [the longest x46 80.9 us: padded_2(): before = lax.ppermute(last, axis, up)]
    slice x89 -> x0, local copies, waits for them, and re-layouts: 57 us -> none  [the longest x15 28.9 us: restrict(): blocks[:, :, 0, :, 1]]
    pallas_call x0 -> x1, Pallas kernels: none -> 53.2 us  [step(): pl.pallas_call(body, out_shape=jax.ShapeDtypeStruct((NZ, R0, C0), F32), i...]
    unnamed x101 -> x11, local copies, waits for them, and re-layouts: 45.9 us -> 5.27 us
    broadcast_in_dim x26 -> x0, local copies, waits for them, and re-layouts: 9.86 us -> none  [the longest x11 6.24 us: build_level(): rim_col[:, :, None]]
    add x23 -> x0, other arithmetic: 5.94 us -> none  [the longest x18 5.85 us: sweep_padded(): return center + DAMPING * (right_side - applied) / level_data[6]]
    convert_element_type x2 -> x0, local copies, waits for them, and re-layouts: 5.4 us -> none  [the longest x1 2.7 us: build_level(): kappa_sq.astype(jnp.float32) + face_x.astype(jnp.float32) + below_x]
  transfers between devices with their start and end apart: 94 -> 0, of which waited for: 44 -> 0; matrix products, arithmetic and copies ran while one was open for 15% -> 0% of each run, Pallas kernels for 0% -> 0%
where the time goes in v1:
time: 58.7 us; the launch traced here: 58.5 us
  Pallas kernels  53.2 us (91%)
  local copies, waits for them, and re-layouts  5.27 us (9%)
    pallas_call x1, Pallas kernels, step(): pl.pallas_call(body, out_shape=jax.ShapeDtypeStruct((NZ, R0, C0), F32), i...  53.2 us
    unnamed x11, local copies, waits for them, and re-layouts  5.27 us

profile of v1, /device:TPU:24, one launch (start us, length us, event | category | flops | bytes accessed | tf_op | source)
XLA Modules:
  0.0 58.5 jit_solution(1476911866443873609)
XLA Ops:
  0.0 0.0 copy-start
  0.0 0.9 %copy-done = f32[8,32,256]{2,1,0:T(8,128)S(1)} copy-done((f32[8,32,256]{2,1,0:T(8,128)S(1)}, f32[8,32,256]{2,1,0:T(8,128)}, u32[]{:S(2)}) %copy-start) | copy-done | bytes 262168
  1.0 0.0 copy-start.1
  1.0 0.9 %copy-done.1 = bf16[8,32,256]{2,1,0:T(8,128)(2,1)S(1)} copy-done((bf16[8,32,256]{2,1,0:T(8,128)(2,1)S(1)}, bf16[8,32,256]{2,1,0:T(8,128)(2,1)}, u32[]{:S(2)}) %copy-start.1) | copy-done | bytes 131096
  1.9 0.0 copy-start.2
  1.9 0.9 %copy-done.2 = bf16[8,32,256]{2,1,0:T(8,128)(2,1)S(1)} copy-done((bf16[8,32,256]{2,1,0:T(8,128)(2,1)S(1)}, bf16[8,32,256]{2,1,0:T(8,128)(2,1)}, u32[]{:S(2)}) %copy-start.2) | copy-done | bytes 131096
  2.8 0.0 copy-start.3
  2.8 0.9 %copy-done.3 = bf16[8,32,256]{2,1,0:T(8,128)(2,1)S(1)} copy-done((bf16[8,32,256]{2,1,0:T(8,128)(2,1)S(1)}, bf16[8,32,256]{2,1,0:T(8,128)(2,1)}, u32[]{:S(2)}) %copy-start.3) | copy-done | bytes 131096
  3.7 0.0 copy-start.4
  3.7 0.9 %copy-done.4 = bf16[8,32,256]{2,1,0:T(8,128)(2,1)S(1)} copy-done((bf16[8,32,256]{2,1,0:T(8,128)(2,1)S(1)}, bf16[8,32,256]{2,1,0:T(8,128)(2,1)}, u32[]{:S(2)}) %copy-start.4) | copy-done | bytes 131096
  4.6 53.2 %shard_map.55 = f32[8,32,256]{2,1,0:T(8,128)S(1)} custom-call(f32[8,32,256]{2,1,0:T(8,128)S(1)} %copy-done, bf16[8,32,256]{2,1,0:T(8,128)(2,1)S(1)} %copy-done.1, bf16[8,32,256]{2,1,0:T(8,128)(2,1)S(1)} %copy-done.2, bf16[8,32,256]{2,1,0:T(8,128)(2,1)S(1)} %copy-done.3, bf16[8,32,256]{2,1,0:T(8,128)(2,1)S(1)} %copy-done.4), custom_call_target="tpu_custom_call" | custom-call | tf_op jit(solution)/shard_map/pallas_call | solution.py:572
  57.7 0.7 %copy.7 = f32[8,32,256]{2,1,0:T(8,128)} copy(f32[8,32,256]{2,1,0:T(8,128)S(1)} %shard_map.55) | data formatting | bytes 524288
Async XLA Ops:
  0.0 0.9 %copy-start = (f32[8,32,256]{2,1,0:T(8,128)S(1)}, f32[8,32,256]{2,1,0:T(8,128)}, u32[]{:S(2)}) copy-start(f32[8,32,256]{2,1,0:T(8,128)} %refs_0_.1) | copy-start | bytes 786436
  1.0 0.9 %copy-start.1 = (bf16[8,32,256]{2,1,0:T(8,128)(2,1)S(1)}, bf16[8,32,256]{2,1,0:T(8,128)(2,1)}, u32[]{:S(2)}) copy-start(bf16[8,32,256]{2,1,0:T(8,128)(2,1)} %refs_1_.1) | copy-start | bytes 393220
  1.9 0.9 %copy-start.2 = (bf16[8,32,256]{2,1,0:T(8,128)(2,1)S(1)}, bf16[8,32,256]{2,1,0:T(8,128)(2,1)}, u32[]{:S(2)}) copy-start(bf16[8,32,256]{2,1,0:T(8,128)(2,1)} %refs_2_.1) | copy-start | bytes 393220
  2.8 0.9 %copy-start.3 = (bf16[8,32,256]{2,1,0:T(8,128)(2,1)S(1)}, bf16[8,32,256]{2,1,0:T(8,128)(2,1)}, u32[]{:S(2)}) copy-start(bf16[8,32,256]{2,1,0:T(8,128)(2,1)} %refs_3_.1) | copy-start | bytes 393220
  3.7 0.9 %copy-start.4 = (bf16[8,32,256]{2,1,0:T(8,128)(2,1)S(1)}, bf16[8,32,256]{2,1,0:T(8,128)(2,1)}, u32[]{:S(2)}) copy-start(bf16[8,32,256]{2,1,0:T(8,128)(2,1)} %refs_4_.1) | copy-start | bytes 393220

commit v2 on v1

--- a/solution.py
+++ b/solution.py
@@ -73,20 +73,15 @@
 
 
 def chunks(lo, hi, step, body):
-    whole = (hi - lo) // step
-    if whole > 1:
-        lax.fori_loop(0, whole, lambda n, c: (body(lo + n * step, step), c)[1], 0)
-    elif whole == 1:
-        body(lo, step)
-    if (hi - lo) % step:
-        body(lo + whole * step, (hi - lo) % step)
+    for i in range(lo, hi, step):
+        body(i, min(step, hi - i))
 
 
 class Level:
     def __init__(self, level, a, d, rd, va, vb):
         self.level, self.a, self.d, self.rd, self.va, self.vb = level, a, d, rd, va, vb
         self.own = OWN[level]
-        self.step = (4, 4, 8, 8, 8, 8)[level]
+        self.step = (38, 44, 24, 12, 26, 12)[level]
 
     def rows(self, ref, i, k):
         return ref[pl.ds(i + self.own, k)]
@@ -192,12 +187,39 @@
     for n in range(6):
         levels.append(Level(n, *get(5)))
     send0, recv0, send1, recv1, sendr, recvr = get(6)
-    send4, recv4, wide4, recv4x = get(4)
+    pack4, side4 = get(2)
     sendv, recvv, widev, recvvx, recv3x = get(5)
-    load_sem, store_sem, ssem, rsem = get(4)
+    load_sem, store_sem, ssem, rsem, known = get(5)
     l0, l1, l2, l3, l4, l5 = levels
 
     mx, my = lax.axis_index("gx"), lax.axis_index("gy")
+
+    def there(dx):
+        if dx == 0:
+            return None
+        return mx + dx < gx if dx > 0 else mx + dx >= 0
+
+    def when(cond, action):
+        if cond is None:
+            action()
+        else:
+            pl.when(cond)(action)
+
+    far = [s * k for k in range(1, REACH + 1) for s in (1, -1)]
+
+    barrier = pltpu.get_barrier_semaphore()
+    partners = [(dx, dy) for dx in (0, 1, -1) for dy in (0, 1, -1) if dx or dy]
+    count = 0
+    for dx in (0, 1, -1):
+        group = [p for p in partners if p[0] == dx]
+
+        def greet(group=group):
+            for px, py in group:
+                ids = (mx + px, lax.rem(my + py + gy, gy))
+                pl.semaphore_signal(barrier, inc=1, device_id=ids, device_id_type=MESH)
+
+        when(there(dx), greet)
+        count = count + (len(group) if dx == 0 else jnp.where(there(dx), len(group), 0))
 
     loads = []
     for h in range(2):
@@ -212,17 +234,6 @@
 
     def plan(name, src, dst, dx, dy):
         transfers[name] = (src, dst, dx, dy, len(transfers))
-
-    def there(dx):
-        if dx == 0:
-            return None
-        return mx + dx < gx if dx > 0 else mx + dx >= 0
-
-    def when(cond, action):
-        if cond is None:
-            action()
-        else:
-            pl.when(cond)(action)
 
     def copy_of(name):
         src, dst, dx, dy, n = transfers[name]
@@ -267,14 +278,25 @@
             plan(("y0", dx, dy), send0.at[e], recv0.at[e, dx + 1], dx, dy)
             plan(("y1", dx, dy), send1.at[e], recv1.at[e, dx + 1], dx, dy)
             plan(("yr", dx, dy), sendr.at[e], recvr.at[e, dx + 1], dx, dy)
-        plan(("y4", dy), send4, recv4.at[e], 0, dy)
+        plan(("y4", dy), pack4, side4.at[e], 0, dy)
         plan(("yv", dy), sendv, recvv.at[e], 0, dy)
-    far = [s * k for k in range(1, REACH + 1) for s in (1, -1)]
     for n, dx in enumerate(far):
-        plan(("x4", dx), wide4, recv4x.at[n], dx, 0)
+        plan(("x4", dx), pack4.at[2 * REACH], pack4.at[n], dx, 0)
         plan(("xv", dx), widev.at[0], recvvx.at[n], dx, 0)
     for n, dx in enumerate((1, -1)):
         plan(("x3", dx), widev.at[pl.ds(1, 4)], recv3x.at[n], dx, 0)
+
+    def tell(word):
+        for e, dx in enumerate((2, -2)):
+
+            def go(e=e, dx=dx):
+                pl.semaphore_signal(known.at[word, e], inc=1, device_id=(mx + dx, my), device_id_type=MESH)
+
+            when(there(dx), go)
+
+    def hear(word):
+        for e, dx in enumerate((2, -2)):
+            when(there(-dx), lambda e=e: pl.semaphore_wait(known.at[word, e], 1))
 
     def zero(ref, *index):
         ref[index] = jnp.zeros(ref[index].shape, F32)
@@ -295,22 +317,8 @@
 
         @pl.when(jnp.logical_not(there(-dx)))
         def _(n=n):
-            recv4x[n] = jnp.zeros((4, NZ, 128), F32)
+            pack4[n] = jnp.zeros((NZ, 128), F32)
             recvvx[n] = jnp.zeros((NZ, 128), F32)
-
-    barrier = pltpu.get_barrier_semaphore()
-    partners = [(0, 1), (0, -1)] + [(dx, 0) for dx in far] + [(dx, dy) for dx in (1, -1) for dy in (1, -1)]
-    count = 0
-    for dx in [0] + far:
-        group = [p for p in partners if p[0] == dx]
-
-        def greet(group=group):
-            for px, py in group:
-                ids = (mx + px, lax.rem(my + py + gy, gy))
-                pl.semaphore_signal(barrier, inc=1, device_id=ids, device_id_type=MESH)
-
-        when(there(dx), greet)
-        count = count + (len(group) if dx == 0 else jnp.where(there(dx), len(group), 0))
 
     for copy in loads:
         copy.wait()
@@ -386,10 +394,13 @@
     l2.coarsen(0, 4, l3)
     l3.coarsen(0, 2, l4)
     lane = lanes_of((NZ, 128))
-    send4[...] = jnp.where(lane < 64, l4.a[1:5, 12], pltpu.roll(l4.a[1:5, 13], 64, 2))
-    send([("y4", 1), ("y4", -1)])
+    total = l4.a[1, 12]
+    for q in range(1, 8):
+        total = jnp.where(lane < 16 * q, total, pltpu.roll(l4.a[1 + q // 2, 12 + q % 2], 16 * q, 1))
+    pack4[2 * REACH] = total
 
     arrive([("x0", 1), ("x0f", 1), ("x0", -1)] + [("y0", *p) for p in sides])
+    tell(0)
     unpack(recv0, l0.a, all_fields, 4, 32, 4, 256, range(-4, 35))
     l0.diagonal(-3, 35)
     l0.first(-3, 35, l0.va)
@@ -408,12 +419,11 @@
         from_l = pltpu.roll(from_l, 128 - size, len(shape) - 1)
         return jnp.where(at < size, own, jnp.where(keep_r, from_r, jnp.where(keep_l, from_l, 0.0)))
 
-    arrive([("y4", 1), ("y4", -1)])
-    wide4[...] = join(send4[...], recv4[0], recv4[1], 16)
-    send([("x4", dx) for dx in far])
 
     arrive([("x1", 1), ("x1", -1)] + [("y1", *p) for p in sides])
     unpack(recv1, l1.a, coefs, 16, 16, 16, 128, range(-15, 30))
+    hear(0)
+    tell(1)
     l1.diagonal(-14, 30)
     l1.coarsen(-7, 15, l2)
     l2.diagonal(-6, 14)
@@ -427,6 +437,8 @@
     l1.first(-14, 30, l1.va)
     l1.sweep(-13, 29, l1.va, l1.vb)
     l1.restrict_residual(-12, 28, l1.vb, l2)
+    hear(1)
+    send([("x4", dx) for dx in far])
     l2.first(-6, 14, l2.va)
     l2.sweep(-5, 13, l2.va, l2.vb)
     l2.restrict_residual(-4, 12, l2.vb, l3)
@@ -448,24 +460,27 @@
         ref[i] = both
         ref[i + 1] = pltpu.roll(both, 64, both.ndim - 1)
 
-    def own_and_far(ref, n_field, i_own):
-        return
-
-    arrive([("x4", dx) for dx in far])
-    for n, dx in list(enumerate(far)) + [(None, 0)]:
-        both = wide4[...] if dx == 0 else recv4x[n]
-        i = 12 - 2 * dx
-        l4.a[1:5, i] = both
-        l4.a[1:5, i + 1] = pltpu.roll(both, 64, 2)
-    l4.diagonal(-11, 13)
-    l4.coarsen(-5, 6, l5, fx_low=-6)
-    l5.diagonal(-5, 6)
-
     arrive([("yv", 1), ("yv", -1)])
     widev[0] = join(sendv[0], recvv[0, 0], recvv[1, 0], 16)
     send([("xv", dx) for dx in far])
     widev[1:5] = join(sendv[1:5], recvv[0, 1:5], recvv[1, 1:5], 32)
     send([("x3", 1), ("x3", -1)])
+
+    arrive([("x4", dx) for dx in far])
+    send([("y4", 1), ("y4", -1)])
+    arrive([("y4", 1), ("y4", -1)])
+    keep_r, keep_l = (lane < 64) & has_right, (lane >= 64) & has_left
+    for n, dx in enumerate(far + [0]):
+        i = 12 - 2 * dx
+        own, from_r, from_l = pack4[n], side4[0, n], side4[1, n]
+        for q in range(8):
+            parts = [pltpu.roll(p, b % 128, 1) if b % 128 else p for p, b in ((own, -16 * q), (from_r, 16 - 16 * q), (from_l, -16 - 16 * q))]
+            row = jnp.where(lane < 16, parts[0], jnp.where(keep_r, parts[1], jnp.where(keep_l, parts[2], 0.0)))
+            l4.a[1 + q // 2, i + q % 2] = row
+    l4.diagonal(-11, 13)
+    l4.coarsen(-5, 6, l5, fx_low=-6)
+    l5.diagonal(-5, 6)
+
     arrive([("xv", dx) for dx in far])
     for n, dx in list(enumerate(far)) + [(None, 0)]:
         spread_two(widev[0] if dx == 0 else recvvx[n], l4.va, 12 - 2 * dx)
@@ -551,10 +566,8 @@
             pltpu.VMEM((2, 3, 2, 4, NZ, 128), F32),
             pltpu.VMEM((2, 2, NZ, 128), F32),
             pltpu.VMEM((2, 3, 2, NZ, 128), F32),
-            pltpu.VMEM((4, NZ, 128), F32),
-            pltpu.VMEM((2, 4, NZ, 128), F32),
-            pltpu.VMEM((4, NZ, 128), F32),
-            pltpu.VMEM((2 * REACH, 4, NZ, 128), F32),
+            pltpu.VMEM((2 * REACH + 1, NZ, 128), F32),
+            pltpu.VMEM((2, 2 * REACH + 1, NZ, 128), F32),
             pltpu.VMEM((5, NZ, 128), F32),
             pltpu.VMEM((2, 5, NZ, 128), F32),
             pltpu.VMEM((5, NZ, 128), F32),
@@ -564,6 +577,7 @@
             pltpu.SemaphoreType.DMA((4, 2)),
             pltpu.SemaphoreType.DMA((number,)),
             pltpu.SemaphoreType.DMA((number,)),
+            pltpu.SemaphoreType.REGULAR((2, 2)),
         ]
 
         def body(*refs):
@@ -576,7 +590,7 @@
             out_specs=pl.BlockSpec(memory_space=pl.ANY),
             scratch_shapes=scratch,
             compiler_params=pltpu.CompilerParams(
-                collective_id=0, has_side_effects=True, vmem_limit_bytes=40 * 2**20
+                collective_id=0, has_side_effects=True, vmem_limit_bytes=60 * 2**20
             ),
         )(*args)
 

time: 58.7 us -> 44.6 us (0.76)
  Pallas kernels: 53.2 us -> 42.8 us
  local copies, waits for them, and re-layouts: 5.27 us -> 1.67 us
    pallas_call x1, Pallas kernels: 53.2 us -> 42.8 us  [step(): pl.pallas_call(body, out_shape=jax.ShapeDtypeStruct((NZ, R0, C0), F32), i...]
    unnamed x11 -> x1, local copies, waits for them, and re-layouts: 5.27 us -> 1.67 us
where the time goes in v2:
time: 44.6 us; the launch traced here: 44.5 us
  Pallas kernels  42.8 us (96%)
  local copies, waits for them, and re-layouts  1.67 us (4%)
    pallas_call x1, Pallas kernels, step(): pl.pallas_call(body, out_shape=jax.ShapeDtypeStruct((NZ, R0, C0), F32), i...  42.8 us
    unnamed x1, local copies, waits for them, and re-layouts  1.67 us

profile of v2, /device:TPU:24, one launch (start us, length us, event | category | flops | bytes accessed | tf_op | source)
XLA Modules:
  0.0 44.5 jit_solution(11694896746371084055)
XLA Ops:
  0.0 42.8 %shard_map.55 = f32[8,32,256]{2,1,0:T(8,128)} custom-call(f32[8,32,256]{2,1,0:T(8,128)} %refs_0_.1, bf16[8,32,256]{2,1,0:T(8,128)(2,1)} %refs_1_.1, bf16[8,32,256]{2,1,0:T(8,128)(2,1)} %refs_2_.1, bf16[8,32,256]{2,1,0:T(8,128)(2,1)} %refs_3_.1, bf16[8,32,256]{2,1,0:T(8,128)(2,1)} %refs_4_.1), custom_call_target="tpu_custom_call" | custom-call | tf_op jit(solution)/shard_map/pallas_call | solution.py:586
  42.8 1.7 %copy.7 = f32[8,32,256]{2,1,0:T(8,128)} copy(f32[8,32,256]{2,1,0:T(8,128)} %shard_map.55) | data formatting | bytes 524288

commit v3 on v2

--- a/solution.py
+++ b/solution.py
@@ -9,10 +9,12 @@
 F32 = jnp.float32
 MESH = pl.DeviceIdType.MESH
 NZ, R0, C0 = 8, 32, 256
-OWN = (4, 16, 8, 4, 12, 6)
-ROWS = (40, 48, 24, 12, 26, 12)
+OWN = (4, 8, 8, 4, 12, 6)
+ROWS = (40, 32, 24, 12, 26, 12)
 LANES = (384, 256, 128, 128, 128, 128)
 REACH = 6
+NSEM = 96
+AROUND = [(dx, dy) for dx in (0, 1, -1) for dy in (0, 1, -1) if dx or dy]
 
 
 def lanes_of(shape):
@@ -81,7 +83,7 @@
     def __init__(self, level, a, d, rd, va, vb):
         self.level, self.a, self.d, self.rd, self.va, self.vb = level, a, d, rd, va, vb
         self.own = OWN[level]
-        self.step = (38, 44, 24, 12, 26, 12)[level]
+        self.step = (38, 32, 24, 12, 26, 12)[level]
 
     def rows(self, ref, i, k):
         return ref[pl.ds(i + self.own, k)]
@@ -102,10 +104,10 @@
     def beside(self, v, i, k):
         c = self.rows(v, i, k)
         fx, fxl, fy, fz = self.field(2, i, k), self.field(2, i - 1, k), self.field(3, i, k), self.field(4, i, k)
-        total = fx * self.rows(v, i + 1, k) + fxl * self.rows(v, i - 1, k)
-        total = total + fy * left(c) + right(fy * c)
-        total = total + fz * above(c) + below(fz * c)
-        return c, total
+        along_x = fx * self.rows(v, i + 1, k) + fxl * self.rows(v, i - 1, k)
+        along_y = fy * left(c) + right(fy * c)
+        along_z = fz * above(c) + below(fz * c)
+        return c, (self.field(0, i, k) + along_x) + (along_y + along_z)
 
     def first(self, lo, hi, out):
         def body(i, k):
@@ -116,7 +118,7 @@
     def sweep(self, lo, hi, v, out):
         def body(i, k):
             c, total = self.beside(v, i, k)
-            new = (1 - DAMPING) * c + self.rows(self.rd, i, k) * (self.field(0, i, k) + total)
+            new = (1 - DAMPING) * c + self.rows(self.rd, i, k) * total
             out[pl.ds(i + self.own, k)] = new
 
         chunks(lo, hi, self.step, body)
@@ -126,7 +128,7 @@
             k = 2 * m
             i = 2 * n
             c, total = self.beside(v, i, k)
-            residual = self.field(0, i, k) - self.rows(self.d, i, k) * c + total
+            residual = total - self.rows(self.d, i, k) * c
             residual = residual[..., : min(residual.shape[-1], 256)]
             residual = residual.reshape(m, 2, *residual.shape[1:])
             coarse.a[0, pl.ds(n + coarse.own, m)] = fit(squeeze_wide(residual[:, 0] + residual[:, 1]) * 0.25, coarse)
@@ -186,9 +188,9 @@
     levels = []
     for n in range(6):
         levels.append(Level(n, *get(5)))
-    send0, recv0, send1, recv1, sendr, recvr = get(6)
-    pack4, side4 = get(2)
-    sendv, recvv, widev, recvvx, recv3x = get(5)
+    send0, recv0, corner, recvc, send1, recv1, sendr, recvr = get(8)
+    send3, recv3, sendk, recvk, send2, recv2 = get(6)
+    pack4, side4, widev, recvvx, recv3x = get(5)
     load_sem, store_sem, ssem, rsem, known = get(5)
     l0, l1, l2, l3, l4, l5 = levels
 
@@ -205,10 +207,10 @@
         else:
             pl.when(cond)(action)
 
-    far = [s * k for k in range(1, REACH + 1) for s in (1, -1)]
+    far = [s * k for k in range(REACH, 0, -1) for s in (1, -1)]
 
     barrier = pltpu.get_barrier_semaphore()
-    partners = [(dx, dy) for dx in (0, 1, -1) for dy in (0, 1, -1) if dx or dy]
+    partners = AROUND
     count = 0
     for dx in (0, 1, -1):
         group = [p for p in partners if p[0] == dx]
@@ -246,13 +248,26 @@
         by = {}
         for name in names:
             by.setdefault(transfers[name][2], []).append(name)
-        for dx, group in by.items():
-
-            def go(group=group):
-                for name in group:
-                    action(copy_of(name))
-
-            when(there(sign * dx), go)
+        reach = max(abs(dx) for dx in by)
+
+        def group(dx):
+            for name in by[dx]:
+                action(copy_of(name))
+
+        def every():
+            for dx in by:
+                group(dx)
+
+        def some():
+            for dx in by:
+                when(there(sign * dx), lambda dx=dx: group(dx))
+
+        if reach == 0:
+            every()
+        else:
+            inside = (mx >= reach) & (mx < gx - reach)
+            pl.when(inside)(every)
+            pl.when(jnp.logical_not(inside))(some)
 
     def send(names):
         grouped(names, lambda c: c.start(), 1)
@@ -260,31 +275,44 @@
     def arrive(names):
         grouped(names, lambda c: c.wait_recv(), -1)
 
-    for d in (1, -1):
-        a0, a1 = l0.a, l1.a
-        s0, t0 = (33, 1) if d == 1 else (4, 36)
-        cols = pl.ds(0, C0)
-        plan(("x0", d), a0.at[:, pl.ds(s0, 3), :, cols], a0.at[:, pl.ds(t0, 3), :, cols], d, 0)
-        if d == 1:
-            plan(("x0f", d), a0.at[2, pl.ds(32, 1), :, cols], a0.at[2, pl.ds(0, 1), :, cols], d, 0)
-        cols = pl.ds(0, 128)
-        s1, t1, n1 = (17, 1, 15) if d == 1 else (16, 32, 14)
-        plan(("x1", d), a1.at[pl.ds(1, 4), pl.ds(s1, n1), :, cols], a1.at[pl.ds(1, 4), pl.ds(t1, n1), :, cols], d, 0)
-        s1, t1 = (18, 2) if d == 1 else (16, 32)
-        plan(("xr", d), a1.at[0, pl.ds(s1, 14), :, cols], a1.at[0, pl.ds(t1, 14), :, cols], d, 0)
-    for dy in (1, -1):
+    a0, a1 = l0.a, l1.a
+    cols, cols1 = pl.ds(0, C0), pl.ds(0, 128)
+
+    def rows0(name, fields, src, dst, rows, d):
+        plan((name, d), a0.at[fields, pl.ds(src, rows), :, cols], a0.at[fields, pl.ds(dst, rows), :, cols], d, 0)
+
+    rows0("x0", pl.ds(0, 5), 34, 2, 2, 1)
+    rows0("x0f", 2, 33, 1, 1, 1)
+    rows0("x0", pl.ds(0, 5), 4, 36, 2, -1)
+    rows0("x0b", pl.ds(0, 2), 33, 1, 1, 1)
+    rows0("x0c", pl.ds(3, 2), 33, 1, 1, 1)
+    rows0("x0d", 2, 32, 0, 1, 1)
+    rows0("x0b", pl.ds(0, 5), 6, 38, 1, -1)
+    for d, src, dst, n1, nr in ((1, 24, 8, 7, 6), (-1, 8, 24, 6, 6)):
+        for name, fields, n in (("x1", pl.ds(1, 4), n1), ("xr", 0, nr)):
+            s_at, d_at = (pl.ds(src - n, n), pl.ds(dst - n, n)) if d == 1 else (pl.ds(src, n), pl.ds(dst, n))
+            plan((name, d), a1.at[fields, s_at, :, cols1], a1.at[fields, d_at, :, cols1], d, 0)
+    for dx, dy in AROUND:
         e = (dy + 1) // 2
-        for dx in (-1, 0, 1):
-            plan(("y0", dx, dy), send0.at[e], recv0.at[e, dx + 1], dx, dy)
+        if dy and dx == 0:
+            plan(("y0", dx, dy), send0.at[e], recv0.at[e], dx, dy)
+        if dy and dx:
+            plan(("c0", dx, dy), corner.at[e, (dx + 1) // 2], recvc.at[e, (dx + 1) // 2], dx, dy)
+        if dy:
             plan(("y1", dx, dy), send1.at[e], recv1.at[e, dx + 1], dx, dy)
             plan(("yr", dx, dy), sendr.at[e], recvr.at[e, dx + 1], dx, dy)
-        plan(("y4", dy), pack4, side4.at[e], 0, dy)
-        plan(("yv", dy), sendv, recvv.at[e], 0, dy)
+        plan(("k3", dx, dy), sendk, recvk.at[dx + 1, dy + 1], dx, dy)
+        plan(("r3", dx, dy), send3, recv3.at[dx + 1, dy + 1], dx, dy)
+        pairs = pl.ds(2 if dx == 1 else 0, 2 if dx else 4)
+        plan(("e2", dx, dy), send2.at[pairs], recv2.at[dx + 1, dy + 1, pairs], dx, dy)
+    for dy in (1, -1):
+        plan(("y4", dy), pack4, side4.at[(dy + 1) // 2], 0, dy)
     for n, dx in enumerate(far):
         plan(("x4", dx), pack4.at[2 * REACH], pack4.at[n], dx, 0)
         plan(("xv", dx), widev.at[0], recvvx.at[n], dx, 0)
     for n, dx in enumerate((1, -1)):
-        plan(("x3", dx), widev.at[pl.ds(1, 4)], recv3x.at[n], dx, 0)
+        plan(("x3", dx), widev.at[pl.ds(1, 2)], recv3x.at[n], dx, 0)
+    assert len(transfers) <= NSEM
 
     def tell(word):
         for e, dx in enumerate((2, -2)):
@@ -304,14 +332,14 @@
     @pl.when(mx == 0)
     def _():
         l0.a[:, 0:4] = jnp.zeros((5, 4, NZ, 384), F32)
-        l1.a[:, 0:16] = jnp.zeros((5, 16, NZ, 256), F32)
-        recv3x[0] = jnp.zeros((4, NZ, 128), F32)
+        l1.a[:, 0:8] = jnp.zeros((5, 8, NZ, 256), F32)
+        recv3x[0] = jnp.zeros((2, NZ, 128), F32)
 
     @pl.when(mx == gx - 1)
     def _():
         l0.a[:, 36:40] = jnp.zeros((5, 4, NZ, 384), F32)
-        l1.a[:, 32:48] = jnp.zeros((5, 16, NZ, 256), F32)
-        recv3x[1] = jnp.zeros((4, NZ, 128), F32)
+        l1.a[:, 24:32] = jnp.zeros((5, 8, NZ, 256), F32)
+        recv3x[1] = jnp.zeros((2, NZ, 128), F32)
 
     for n, dx in enumerate(far):
 
@@ -341,12 +369,7 @@
             for f in range(4):
                 l0.a[1 + f, 4 + i, :, cols] = wide.at[h, f][pl.ds(i, NZ, stride=32), :]
 
-    edge = [0, 1, 2, 28, 29, 30, 31]
-    for i in edge:
-        turn(i)
-    pl.semaphore_wait(barrier, count)
-    send([("x0", 1), ("x0f", 1), ("x0", -1)])
-    for i in range(3, 28):
+    for i in range(R0):
         turn(i)
 
     def pack(a, fields, own, count, width, last, dst):
@@ -365,109 +388,185 @@
 
     has_left, has_right = my > 0, my < gy - 1
 
-    def unpack(src, a, fields, own, count, width, last, rows):
-        per = 128 // width
+    def unpack(part, a, fields, own, count, width, last, rows):
         lane = lanes_of((NZ, 128))
         for i in rows:
             dx = -1 if i < 0 else (1 if i >= count else 0)
-            j = i - dx * count
             keep_r, keep_l = has_right, has_left
             if dx:
                 keep_r, keep_l = keep_r & there(dx), keep_l & there(dx)
-            from_r, from_l = src[0, 1 - dx, j // per], src[1, 1 - dx, j // per]
-            shift = (128 - width * (j % per)) % 128
-            from_r = pltpu.roll(from_r, shift, from_r.ndim - 1) if shift else from_r
-            shift = (shift + 128 - width) % 128
-            from_l = pltpu.roll(from_l, shift, from_l.ndim - 1) if shift else from_l
-            row = jnp.where((lane < width) & keep_r, from_r, jnp.where((lane >= 128 - width) & keep_l, from_l, 0.0))
+            sides = []
+            for e in range(2):
+                values, place = part(e, dx, i - dx * count)
+                shift = (128 - width * (place + e)) % 128
+                sides.append(pltpu.roll(values, shift, values.ndim - 1) if shift else values)
+            row = jnp.where((lane < width) & keep_r, sides[0], jnp.where((lane >= 128 - width) & keep_l, sides[1], 0.0))
             a[fields, own + i, :, pl.ds(last, 128)] = row
 
     all_fields, coefs = slice(0, 5), slice(1, 5)
-    sides = [(dx, dy) for dy in (1, -1) for dx in (0, -1, 1)]
+    lane = lanes_of((NZ, 128))
+    sides = [p for p in AROUND if p[1]]
+
+    def names(name, places=AROUND):
+        return [(name, *p) for p in places]
+
     pack(l0.a, all_fields, 4, 32, 4, 128, send0)
-    send([("y0", *p) for p in sides])
-
+    for e in range(2):
+        for d in range(2):
+            total = None
+            for f in range(5):
+                shift = (16 * f - (112 if d else 0)) % 128
+                part = send0[e, 0, f]
+                part = pltpu.roll(part, shift, 1) if shift else part
+                total = part if total is None else jnp.where(lane < 16 * f, total, part)
+            corner[e, d] = total
     l0.coarsen(0, 16, l1)
-    pack(l1.a, coefs, 16, 16, 16, 0, send1)
-    send([("x1", 1), ("x1", -1)] + [("y1", *p) for p in sides])
+    pack(l1.a, coefs, 8, 16, 8, 0, send1)
+    pl.semaphore_wait(barrier, count)
+    first = [("x0", 1), ("x0f", 1), ("x0", -1)] + names("y0", [(0, 1), (0, -1)]) + names("c0", [p for p in sides if p[0]])
+    send(first)
+
+    second = [("x1", 1), ("x1", -1)] + names("y1", sides)
+    send(second)
     l1.coarsen(0, 8, l2)
     l2.coarsen(0, 4, l3)
+
+    def pack3(row):
+        total = row(0)
+        for j in range(1, 4):
+            part = row(j)
+            total = jnp.where(lane < 32 * j, total, pltpu.roll(part, 32 * j, part.ndim - 1))
+        return total
+
+    sendk[...] = pack3(lambda j: l3.a[1:5, 4 + j])
+    send(names("k3"))
     l3.coarsen(0, 2, l4)
-    lane = lanes_of((NZ, 128))
     total = l4.a[1, 12]
     for q in range(1, 8):
         total = jnp.where(lane < 16 * q, total, pltpu.roll(l4.a[1 + q // 2, 12 + q % 2], 16 * q, 1))
     pack4[2 * REACH] = total
 
-    arrive([("x0", 1), ("x0f", 1), ("x0", -1)] + [("y0", *p) for p in sides])
+    def part0(e, dx, j):
+        if dx == 0:
+            return recv0[e, 0], j
+        j = j - 28 if dx < 0 else j
+        values = recvc[e, (1 - dx) // 2]
+        return jnp.stack([pltpu.roll(values, 128 - 16 * f, 1) if f else values for f in range(5)]), j
+
+    beside = first[3:5]
+    arrive(beside)
+    unpack(part0, l0.a, all_fields, 4, 32, 4, 256, range(32))
+    l0.diagonal(1, 32)
+    l0.first(1, 32, l0.va)
+    l0.sweep(2, 31, l0.va, l0.vb)
+    l0.restrict_residual(4, 30, l0.vb, l1)
+    arrive(first[:3] + first[5:])
     tell(0)
-    unpack(recv0, l0.a, all_fields, 4, 32, 4, 256, range(-4, 35))
-    l0.diagonal(-3, 35)
-    l0.first(-3, 35, l0.va)
-    l0.sweep(-2, 34, l0.va, l0.vb)
-    l0.restrict_residual(0, 32, l0.vb, l1)
-    send([("xr", 1), ("xr", -1)])
-    pack(l1.a, 0, 16, 16, 16, 0, sendr)
-    send([("yr", *p) for p in sides])
-
-    def join(own, from_r, from_l, size):
-        shape = own.shape
-        at = lanes_of(shape) & 63
-        keep_r = (at >= size) & (at < 48) & has_right
-        keep_l = (at >= 48) & has_left
-        from_r = pltpu.roll(from_r, size, len(shape) - 1)
-        from_l = pltpu.roll(from_l, 128 - size, len(shape) - 1)
-        return jnp.where(at < size, own, jnp.where(keep_r, from_r, jnp.where(keep_l, from_l, 0.0)))
-
-
-    arrive([("x1", 1), ("x1", -1)] + [("y1", *p) for p in sides])
-    unpack(recv1, l1.a, coefs, 16, 16, 16, 128, range(-15, 30))
+    unpack(part0, l0.a, all_fields, 4, 32, 4, 256, [*range(-4, 0), *range(32, 35)])
+    for lo, hi in ((-2, 1), (32, 34)):
+        l0.diagonal(lo, hi)
+    for lo, hi in ((-2, 1), (32, 34)):
+        l0.first(lo, hi, l0.va)
+    for lo, hi in ((-1, 2), (31, 33)):
+        l0.sweep(lo, hi, l0.va, l0.vb)
+    for lo, hi in ((0, 4), (30, 32)):
+        l0.restrict_residual(lo, hi, l0.vb, l1)
+    pack(l1.a, 0, 8, 16, 8, 0, sendr)
+    third = [("xr", 1), ("xr", -1)] + names("yr", sides)
+    send(third)
+    later = [("x0b", 1), ("x0c", 1), ("x0d", 1), ("x0b", -1)]
+    send(later)
+
+    arrive(second)
     hear(0)
     tell(1)
-    l1.diagonal(-14, 30)
-    l1.coarsen(-7, 15, l2)
-    l2.diagonal(-6, 14)
-    l2.coarsen(-3, 7, l3, fx_low=-4)
+    unpack(lambda e, dx, j: (recv1[e, 1 - dx, 0], j), l1.a, coefs, 8, 16, 8, 128, range(-7, 22))
+    l1.diagonal(-6, 22)
+    l1.coarsen(-3, 11, l2, fx_low=-4)
+    l2.diagonal(-3, 11)
+
+    def spread3(own, src, a, fields):
+        for px in (-1, 0, 1):
+            mid, from_r, from_l = own if px == 0 else src[1 - px, 1], src[1 - px, 0], src[1 - px, 2]
+            for j in range(4):
+                parts = []
+                for values, shift in ((mid, -32 * j), (from_r, 32 - 32 * j), (from_l, 96 - 32 * j)):
+                    parts.append(pltpu.roll(values, shift % 128, values.ndim - 1) if shift % 128 else values)
+                row = jnp.where((lane < 64) & has_right, parts[1], jnp.where((lane >= 96) & has_left, parts[2], 0.0))
+                row = jnp.where(lane < 32, parts[0], row)
+                if px:
+                    row = jnp.where(there(px), row, 0.0)
+                a[fields, 4 + 4 * px + j] = row
+
+    arrive(names("k3"))
+    spread3(sendk[...], recvk, l3.a, coefs)
     l3.diagonal(-3, 7)
     l3.coarsen(-1, 2, l4)
     l4.diagonal(0, 2)
 
-    arrive([("xr", 1), ("xr", -1)] + [("yr", *p) for p in sides])
-    unpack(recvr, l1.a, 0, 16, 16, 16, 128, range(-14, 30))
-    l1.first(-14, 30, l1.va)
-    l1.sweep(-13, 29, l1.va, l1.vb)
-    l1.restrict_residual(-12, 28, l1.vb, l2)
+    arrive(third)
+    unpack(lambda e, dx, j: (recvr[e, 1 - dx, 0], j), l1.a, 0, 8, 16, 8, 128, range(-6, 22))
+    l1.first(-6, 22, l1.va)
+    l1.sweep(-5, 21, l1.va, l1.vb)
+    l1.restrict_residual(-4, 20, l1.vb, l2)
+    l2.first(-2, 10, l2.va)
+    l2.sweep(-1, 9, l2.va, l2.vb)
+    l2.restrict_residual(0, 8, l2.vb, l3)
+
+    send3[...] = pack3(lambda j: l3.a[0, 4 + j])
+    send(names("r3"))
+    for n in range(4):
+        send2[n, 0] = jnp.where(lane < 64, l2.a[0, 8 + 2 * n], pltpu.roll(l2.a[0, 9 + 2 * n], 64, 1))
+        send2[n, 1] = jnp.where(lane < 64, l2.vb[8 + 2 * n], pltpu.roll(l2.vb[9 + 2 * n], 64, 1))
     hear(1)
     send([("x4", dx) for dx in far])
-    l2.first(-6, 14, l2.va)
-    l2.sweep(-5, 13, l2.va, l2.vb)
-    l2.restrict_residual(-4, 12, l2.vb, l3)
+    send(names("e2"))
+
+    arrive(names("r3"))
+    spread3(send3[...], recv3, l3.a, 0)
     l3.first(-2, 6, l3.va)
     l3.sweep(-1, 5, l3.va, l3.vb)
     l3.restrict_residual(0, 4, l3.vb, l4)
     l4.first(0, 2, l4.va)
 
     def two(ref, i):
-        return jnp.where(lane < 64, ref[i], pltpu.roll(ref[i + 1], 64, 1))
-
-    sendv[0] = two(l4.va, 12)
+        return jnp.where((lane < 48) | (lane >= 112), ref[i], pltpu.roll(ref[i + 1], 64, 1))
+
+    widev[0] = two(l4.va, 12)
+    send([("xv", dx) for dx in far])
     for n in range(2):
-        sendv[1 + n] = two(l3.a.at[0], 4 + 2 * n)
-        sendv[3 + n] = two(l3.vb, 4 + 2 * n)
-    send([("yv", 1), ("yv", -1)])
+        widev[1 + n] = two(l3.vb, 4 + 2 * n)
+    send([("x3", 1), ("x3", -1)])
 
     def spread_two(both, ref, i):
         ref[i] = both
         ref[i + 1] = pltpu.roll(both, 64, both.ndim - 1)
 
-    arrive([("yv", 1), ("yv", -1)])
-    widev[0] = join(sendv[0], recvv[0, 0], recvv[1, 0], 16)
-    send([("xv", dx) for dx in far])
-    widev[1:5] = join(sendv[1:5], recvv[0, 1:5], recvv[1, 1:5], 32)
-    send([("x3", 1), ("x3", -1)])
-
     arrive([("x4", dx) for dx in far])
     send([("y4", 1), ("y4", -1)])
+
+    arrive(later)
+    for lo, hi in ((-3, -2), (34, 35)):
+        l0.diagonal(lo, hi)
+        l0.first(lo, hi, l0.va)
+    for lo, hi in ((-2, -1), (33, 34)):
+        l0.sweep(lo, hi, l0.va, l0.vb)
+    arrive(names("e2"))
+    for px in (-1, 0, 1):
+        for n in (range(2, 4) if px < 0 else range(2) if px else range(4)):
+            mid = send2[n] if px == 0 else recv2[1 - px, 1, n]
+            from_r, from_l = recv2[1 - px, 0, n], recv2[1 - px, 2, n]
+            zero = jnp.zeros_like(mid)
+            from_r, from_l = jnp.where(has_right, from_r, zero), jnp.where(has_left, from_l, zero)
+            even = jnp.where(lane < 64, mid, pltpu.roll(jnp.where(lane < 32, from_r, from_l), 64, 2))
+            odd = jnp.where(lane < 64, pltpu.roll(mid, 64, 2), jnp.where(lane < 96, from_r, from_l))
+            for j, row in enumerate((even, odd)):
+                if px:
+                    row = jnp.where(there(px), row, zero)
+                i = 8 + 8 * px + 2 * n + j
+                l2.a[0, i] = row[0]
+                l2.vb[i] = row[1]
+
     arrive([("y4", 1), ("y4", -1)])
     keep_r, keep_l = (lane < 64) & has_right, (lane >= 64) & has_left
     for n, dx in enumerate(far + [0]):
@@ -480,6 +579,8 @@
     l4.diagonal(-11, 13)
     l4.coarsen(-5, 6, l5, fx_low=-6)
     l5.diagonal(-5, 6)
+    late = ("xv", "x3")
+    grouped([n for n in transfers if n[0] not in late], lambda c: c.wait_send(), 1)
 
     arrive([("xv", dx) for dx in far])
     for n, dx in list(enumerate(far)) + [(None, 0)]:
@@ -502,11 +603,9 @@
     l4.sweep(-2, 4, l4.vb, l4.va)
 
     arrive([("x3", 1), ("x3", -1)])
-    for src, dx in ((widev.at[pl.ds(1, 4)], 0), (recv3x.at[0], 1), (recv3x.at[1], -1)):
+    for src, dx in ((recv3x.at[0], 1), (recv3x.at[1], -1)):
         for n in range(2):
-            i = 4 - 4 * dx + 2 * n
-            spread_two(src[n], l3.a.at[0], i)
-            spread_two(src[2 + n], l3.vb, i)
+            spread_two(src[n], l3.vb, 4 - 4 * dx + 2 * n)
     l3.correct(-4, 8, l3.vb, l4, l4.va, l3.va)
     l3.sweep(-3, 7, l3.va, l3.vb)
     l3.sweep(-2, 6, l3.vb, l3.va)
@@ -526,7 +625,7 @@
         for q in range(2):
             i = 8 * n + 4 * q
             mid, total = l0.beside(l0.vb, i, 4)
-            new = (1 - DAMPING) * mid + l0.rows(l0.rd, i, 4) * (l0.field(0, i, 4) + total)
+            new = (1 - DAMPING) * mid + l0.rows(l0.rd, i, 4) * total
             for j in range(4):
                 for h in range(2):
                     out_v.at[h].reshape(256, 128)[pl.ds(i + j, NZ, stride=32), :] = new[j, :, 128 * h : 128 * h + 128]
@@ -538,7 +637,7 @@
             rows, cols = pl.ds(8 * n, 8), pl.ds(128 * h, 128)
             pltpu.make_async_copy(out_v.at[h, :, rows], field.at[:, rows, cols], store_sem.at[n, h]).start()
 
-    grouped(list(transfers), lambda c: c.wait_send(), 1)
+    grouped([n for n in transfers if n[0] in late], lambda c: c.wait_send(), 1)
     for n in range(4):
         for h in range(2):
             rows, cols = pl.ds(8 * n, 8), pl.ds(128 * h, 128)
@@ -547,8 +646,6 @@
 
 def solution(mesh):
     gx, gy = mesh.shape["gx"], mesh.shape["gy"]
-    number = 2 + 1 + 2 + 2 + 18 + 4 + 4 * REACH + 2
-
     def step(*args):
         scratch = [
             pltpu.VMEM((2, NZ, R0, 128), F32),
@@ -561,22 +658,28 @@
             scratch += [pltpu.VMEM((rows, NZ, cols), F32)] * 4
         scratch += [
             pltpu.VMEM((2, 1, 5, NZ, 128), F32),
-            pltpu.VMEM((2, 3, 1, 5, NZ, 128), F32),
-            pltpu.VMEM((2, 2, 4, NZ, 128), F32),
-            pltpu.VMEM((2, 3, 2, 4, NZ, 128), F32),
+            pltpu.VMEM((2, 1, 5, NZ, 128), F32),
             pltpu.VMEM((2, 2, NZ, 128), F32),
-            pltpu.VMEM((2, 3, 2, NZ, 128), F32),
+            pltpu.VMEM((2, 2, NZ, 128), F32),
+            pltpu.VMEM((2, 1, 4, NZ, 128), F32),
+            pltpu.VMEM((2, 3, 1, 4, NZ, 128), F32),
+            pltpu.VMEM((2, 1, NZ, 128), F32),
+            pltpu.VMEM((2, 3, 1, NZ, 128), F32),
+            pltpu.VMEM((NZ, 128), F32),
+            pltpu.VMEM((3, 3, NZ, 128), F32),
+            pltpu.VMEM((4, NZ, 128), F32),
+            pltpu.VMEM((3, 3, 4, NZ, 128), F32),
+            pltpu.VMEM((4, 2, NZ, 128), F32),
+            pltpu.VMEM((3, 3, 4, 2, NZ, 128), F32),
             pltpu.VMEM((2 * REACH + 1, NZ, 128), F32),
             pltpu.VMEM((2, 2 * REACH + 1, NZ, 128), F32),
-            pltpu.VMEM((5, NZ, 128), F32),
-            pltpu.VMEM((2, 5, NZ, 128), F32),
-            pltpu.VMEM((5, NZ, 128), F32),
+            pltpu.VMEM((3, NZ, 128), F32),
             pltpu.VMEM((2 * REACH, NZ, 128), F32),
-            pltpu.VMEM((2, 4, NZ, 128), F32),
+            pltpu.VMEM((2, 2, NZ, 128), F32),
             pltpu.SemaphoreType.DMA((2, 5)),
             pltpu.SemaphoreType.DMA((4, 2)),
-            pltpu.SemaphoreType.DMA((number,)),
-            pltpu.SemaphoreType.DMA((number,)),
+            pltpu.SemaphoreType.DMA((NSEM,)),
+            pltpu.SemaphoreType.DMA((NSEM,)),
             pltpu.SemaphoreType.REGULAR((2, 2)),
         ]
 

time: 44.6 us -> 41.4 us (0.928)
  Pallas kernels: 42.8 us -> 39.2 us
    pallas_call x1, Pallas kernels: 42.8 us -> 39.2 us  [step(): pl.pallas_call(body, out_shape=jax.ShapeDtypeStruct((NZ, R0, C0), F32), i...]
where the time goes in v3:
time: 41.4 us; the launch traced here: 40.9 us
  Pallas kernels  39.2 us (95%)
  local copies, waits for them, and re-layouts  1.67 us (4%)
    pallas_call x1, Pallas kernels, step(): pl.pallas_call(body, out_shape=jax.ShapeDtypeStruct((NZ, R0, C0), F32), i...  39.2 us
    unnamed x1, local copies, waits for them, and re-layouts  1.67 us

profile of v3, /device:TPU:24, one launch (start us, length us, event | category | flops | bytes accessed | tf_op | source)
XLA Modules:
  0.0 40.9 jit_solution(6348385036367758246)
XLA Ops:
  0.0 39.2 %shard_map.55 = f32[8,32,256]{2,1,0:T(8,128)} custom-call(f32[8,32,256]{2,1,0:T(8,128)} %refs_0_.1, bf16[8,32,256]{2,1,0:T(8,128)(2,1)} %refs_1_.1, bf16[8,32,256]{2,1,0:T(8,128)(2,1)} %refs_2_.1, bf16[8,32,256]{2,1,0:T(8,128)(2,1)} %refs_3_.1, bf16[8,32,256]{2,1,0:T(8,128)(2,1)} %refs_4_.1), custom_call_target="tpu_custom_call" | custom-call | tf_op jit(solution)/shard_map/pallas_call | solution.py:689
  39.2 1.7 %copy.7 = f32[8,32,256]{2,1,0:T(8,128)} copy(f32[8,32,256]{2,1,0:T(8,128)} %shard_map.55) | data formatting | bytes 524288

commit v4 on v3

--- a/solution.py
+++ b/solution.py
@@ -122,6 +122,41 @@
             out[pl.ds(i + self.own, k)] = new
 
         chunks(lo, hi, self.step, body)
+
+    def beside_values(self, v, lo):
+        c, k = v[1:-1], v.shape[0] - 2
+        fx, fxl, fy, fz = self.field(2, lo, k), self.field(2, lo - 1, k), self.field(3, lo, k), self.field(4, lo, k)
+        along_x = fx * v[2:] + fxl * v[:-2]
+        along_y = fy * left(c) + right(fy * c)
+        along_z = fz * above(c) + below(fz * c)
+        return c, (self.field(0, lo, k) + along_x) + (along_y + along_z)
+
+    def first_values(self, lo, hi):
+        return self.rows(self.rd, lo, hi - lo) * self.field(0, lo, hi - lo)
+
+    def sweep_values(self, v, lo):
+        c, total = self.beside_values(v, lo)
+        return (1 - DAMPING) * c + self.rows(self.rd, lo, c.shape[0]) * total
+
+    def down(self, lo, hi, v, coarse):
+        v = self.sweep_values(v, lo + 1)
+        self.vb[pl.ds(lo + 1 + self.own, v.shape[0])] = v
+        c, total = self.beside_values(v, lo + 2)
+        residual = total - self.rows(self.d, lo + 2, c.shape[0]) * c
+        m = c.shape[0] // 2
+        residual = residual.reshape(m, 2, *residual.shape[1:])
+        coarse.a[0, pl.ds((lo + 2) // 2 + coarse.own, m)] = squeeze_wide(residual[:, 0] + residual[:, 1]) * 0.25
+
+    def up(self, v, lo, hi, cut=0):
+        m = v.shape[0]
+        if self.level == 1:
+            parts = [take(v, stretch_index("low")), take(v, stretch_index("high"))]
+        else:
+            parts = [take(v, stretch_index("late"))]
+        parts = [jnp.broadcast_to(p[:, None], (m, 2, NZ, 128)).reshape(2 * m, NZ, 128) for p in parts]
+        v = self.rows(self.vb, lo, hi - lo) + (parts[0] if len(parts) == 1 else jnp.concatenate(parts, axis=2))
+        v = v[cut : v.shape[0] - cut]
+        return self.sweep_values(self.sweep_values(v, lo + cut + 1), lo + cut + 2)
 
     def restrict_residual(self, lo, hi, v, coarse):
         def body(n, m):
@@ -315,7 +350,7 @@
     assert len(transfers) <= NSEM
 
     def tell(word):
-        for e, dx in enumerate((2, -2)):
+        for e, dx in enumerate((1, -1) if word == 0 else (2, -2)):
 
             def go(e=e, dx=dx):
                 pl.semaphore_signal(known.at[word, e], inc=1, device_id=(mx + dx, my), device_id_type=MESH)
@@ -323,7 +358,7 @@
             when(there(dx), go)
 
     def hear(word):
-        for e, dx in enumerate((2, -2)):
+        for e, dx in enumerate((1, -1) if word == 0 else (2, -2)):
             when(there(-dx), lambda e=e: pl.semaphore_wait(known.at[word, e], 1))
 
     def zero(ref, *index):
@@ -410,6 +445,9 @@
     def names(name, places=AROUND):
         return [(name, *p) for p in places]
 
+    first = [("x0", 1), ("x0f", 1), ("x0", -1)] + names("y0", [(0, 1), (0, -1)]) + names("c0", [p for p in sides if p[0]])
+    pl.semaphore_wait(barrier, count)
+    send(first[:3])
     pack(l0.a, all_fields, 4, 32, 4, 128, send0)
     for e in range(2):
         for d in range(2):
@@ -420,14 +458,14 @@
                 part = pltpu.roll(part, shift, 1) if shift else part
                 total = part if total is None else jnp.where(lane < 16 * f, total, part)
             corner[e, d] = total
+    first = [("x0", 1), ("x0f", 1), ("x0", -1)] + names("y0", [(0, 1), (0, -1)]) + names("c0", [p for p in sides if p[0]])
+    send(first[3:])
     l0.coarsen(0, 16, l1)
     pack(l1.a, coefs, 8, 16, 8, 0, send1)
-    pl.semaphore_wait(barrier, count)
-    first = [("x0", 1), ("x0f", 1), ("x0", -1)] + names("y0", [(0, 1), (0, -1)]) + names("c0", [p for p in sides if p[0]])
-    send(first)
 
     second = [("x1", 1), ("x1", -1)] + names("y1", sides)
     send(second)
+    tell(0)
     l1.coarsen(0, 8, l2)
     l2.coarsen(0, 4, l3)
 
@@ -454,14 +492,25 @@
         return jnp.stack([pltpu.roll(values, 128 - 16 * f, 1) if f else values for f in range(5)]), j
 
     beside = first[3:5]
+    hear(0)
+    tell(1)
     arrive(beside)
     unpack(part0, l0.a, all_fields, 4, 32, 4, 256, range(32))
     l0.diagonal(1, 32)
     l0.first(1, 32, l0.va)
     l0.sweep(2, 31, l0.va, l0.vb)
     l0.restrict_residual(4, 30, l0.vb, l1)
+    close = names("y1", [(0, 1), (0, -1)])
+    arrive(close)
+
+    def part1(e, dx, j):
+        return recv1[e, 1 - dx, 0], j
+
+    unpack(part1, l1.a, coefs, 8, 16, 8, 128, range(16))
+    l1.diagonal(1, 16)
+    hear(1)
+    tell(2)
     arrive(first[:3] + first[5:])
-    tell(0)
     unpack(part0, l0.a, all_fields, 4, 32, 4, 256, [*range(-4, 0), *range(32, 35)])
     for lo, hi in ((-2, 1), (32, 34)):
         l0.diagonal(lo, hi)
@@ -475,13 +524,11 @@
     third = [("xr", 1), ("xr", -1)] + names("yr", sides)
     send(third)
     later = [("x0b", 1), ("x0c", 1), ("x0d", 1), ("x0b", -1)]
-    send(later)
-
-    arrive(second)
-    hear(0)
-    tell(1)
-    unpack(lambda e, dx, j: (recv1[e, 1 - dx, 0], j), l1.a, coefs, 8, 16, 8, 128, range(-7, 22))
-    l1.diagonal(-6, 22)
+
+    arrive([n for n in second if n not in close])
+    unpack(part1, l1.a, coefs, 8, 16, 8, 128, [*range(-7, 0), *range(16, 22)])
+    l1.diagonal(-6, 1)
+    l1.diagonal(16, 22)
     l1.coarsen(-3, 11, l2, fx_low=-4)
     l2.diagonal(-3, 11)
 
@@ -498,35 +545,29 @@
                     row = jnp.where(there(px), row, 0.0)
                 a[fields, 4 + 4 * px + j] = row
 
+    hear(2)
+    send([("x4", dx) for dx in far])
+    arrive(third)
+    unpack(lambda e, dx, j: (recvr[e, 1 - dx, 0], j), l1.a, 0, 8, 16, 8, 128, range(-6, 22))
+    l1.down(-6, 22, l1.first_values(-6, 22), l2)
+    l2.down(-2, 10, l2.first_values(-2, 10), l3)
+
+    send3[...] = pack3(lambda j: l3.a[0, 4 + j])
+    send(names("r3"))
+    for n in range(4):
+        send2[n, 0] = jnp.where(lane < 64, l2.a[0, 8 + 2 * n], pltpu.roll(l2.a[0, 9 + 2 * n], 64, 1))
+        send2[n, 1] = jnp.where(lane < 64, l2.vb[8 + 2 * n], pltpu.roll(l2.vb[9 + 2 * n], 64, 1))
+    send(names("e2"))
+    send(later)
     arrive(names("k3"))
     spread3(sendk[...], recvk, l3.a, coefs)
     l3.diagonal(-3, 7)
     l3.coarsen(-1, 2, l4)
     l4.diagonal(0, 2)
 
-    arrive(third)
-    unpack(lambda e, dx, j: (recvr[e, 1 - dx, 0], j), l1.a, 0, 8, 16, 8, 128, range(-6, 22))
-    l1.first(-6, 22, l1.va)
-    l1.sweep(-5, 21, l1.va, l1.vb)
-    l1.restrict_residual(-4, 20, l1.vb, l2)
-    l2.first(-2, 10, l2.va)
-    l2.sweep(-1, 9, l2.va, l2.vb)
-    l2.restrict_residual(0, 8, l2.vb, l3)
-
-    send3[...] = pack3(lambda j: l3.a[0, 4 + j])
-    send(names("r3"))
-    for n in range(4):
-        send2[n, 0] = jnp.where(lane < 64, l2.a[0, 8 + 2 * n], pltpu.roll(l2.a[0, 9 + 2 * n], 64, 1))
-        send2[n, 1] = jnp.where(lane < 64, l2.vb[8 + 2 * n], pltpu.roll(l2.vb[9 + 2 * n], 64, 1))
-    hear(1)
-    send([("x4", dx) for dx in far])
-    send(names("e2"))
-
     arrive(names("r3"))
     spread3(send3[...], recv3, l3.a, 0)
-    l3.first(-2, 6, l3.va)
-    l3.sweep(-1, 5, l3.va, l3.vb)
-    l3.restrict_residual(0, 4, l3.vb, l4)
+    l3.down(-2, 6, l3.first_values(-2, 6), l4)
     l4.first(0, 2, l4.va)
 
     def two(ref, i):
@@ -567,6 +608,8 @@
                 l2.a[0, i] = row[0]
                 l2.vb[i] = row[1]
 
+    late = ("xv", "x3", "x4", "y4")
+    grouped([n for n in transfers if n[0] not in late], lambda c: c.wait_send(), 1)
     arrive([("y4", 1), ("y4", -1)])
     keep_r, keep_l = (lane < 64) & has_right, (lane >= 64) & has_left
     for n, dx in enumerate(far + [0]):
@@ -579,44 +622,27 @@
     l4.diagonal(-11, 13)
     l4.coarsen(-5, 6, l5, fx_low=-6)
     l5.diagonal(-5, 6)
-    late = ("xv", "x3")
-    grouped([n for n in transfers if n[0] not in late], lambda c: c.wait_send(), 1)
 
     arrive([("xv", dx) for dx in far])
     for n, dx in list(enumerate(far)) + [(None, 0)]:
         spread_two(widev[0] if dx == 0 else recvvx[n], l4.va, 12 - 2 * dx)
 
-    def body(i, k):
-        l4.a[0, pl.ds(i + 12, k)] = l4.rows(l4.va, i, k) * l4.rows(l4.d, i, k) * (1 / DAMPING)
-
-    chunks(-11, 13, 8, body)
-    l4.sweep(-11, 13, l4.va, l4.vb)
-    l4.restrict_residual(-10, 12, l4.vb, l5)
-
-    l5.first(-5, 6, l5.va)
-    l5.sweep(-4, 5, l5.va, l5.vb)
-    l5.sweep(-3, 4, l5.vb, l5.va)
-    l5.sweep(-2, 3, l5.va, l5.vb)
-
-    l4.correct(-4, 6, l4.vb, l5, l5.vb, l4.va)
-    l4.sweep(-3, 5, l4.va, l4.vb)
-    l4.sweep(-2, 4, l4.vb, l4.va)
-
+    v = l4.rows(l4.va, -12, 26)
+    l4.a[0, pl.ds(1, 24)] = v[1:25] * l4.rows(l4.d, -11, 24) * (1 / DAMPING)
+    l4.down(-12, 14, v, l5)
+
+    v = l5.first_values(-5, 6)
+    for lo in (-4, -3, -2):
+        v = l5.sweep_values(v, lo)
+
+    v = l4.up(v, -4, 6)
     arrive([("x3", 1), ("x3", -1)])
     for src, dx in ((recv3x.at[0], 1), (recv3x.at[1], -1)):
         for n in range(2):
             spread_two(src[n], l3.vb, 4 - 4 * dx + 2 * n)
-    l3.correct(-4, 8, l3.vb, l4, l4.va, l3.va)
-    l3.sweep(-3, 7, l3.va, l3.vb)
-    l3.sweep(-2, 6, l3.vb, l3.va)
-
-    l2.correct(-4, 12, l2.vb, l3, l3.va, l2.va)
-    l2.sweep(-3, 11, l2.va, l2.vb)
-    l2.sweep(-2, 10, l2.vb, l2.va)
-
-    l1.correct(-4, 20, l1.vb, l2, l2.va, l1.va)
-    l1.sweep(-2, 18, l1.va, l1.vb)
-    l1.sweep(-1, 17, l1.vb, l1.va)
+    v = l3.up(v, -4, 8)
+    v = l2.up(v, -4, 12)
+    l1.va[pl.ds(l1.own - 1, 18)] = l1.up(v, -4, 20, 1)
 
     l0.correct(-2, 34, l0.vb, l1, l1.va, l0.va)
     l0.sweep(-1, 33, l0.va, l0.vb)
@@ -680,7 +706,7 @@
             pltpu.SemaphoreType.DMA((4, 2)),
             pltpu.SemaphoreType.DMA((NSEM,)),
             pltpu.SemaphoreType.DMA((NSEM,)),
-            pltpu.SemaphoreType.REGULAR((2, 2)),
+            pltpu.SemaphoreType.REGULAR((3, 2)),
         ]
 
         def body(*refs):

time: 41.4 us -> 40.4 us (0.976)
  Pallas kernels: 39.2 us -> 38.5 us
    pallas_call x1, Pallas kernels: 39.2 us -> 38.5 us  [step(): pl.pallas_call(body, out_shape=jax.ShapeDtypeStruct((NZ, R0, C0), F32), i...]
where the time goes in v4:
time: 40.4 us; the launch traced here: 40.2 us
  Pallas kernels  38.5 us (95%)
  local copies, waits for them, and re-layouts  1.67 us (4%)
    pallas_call x1, Pallas kernels, step(): pl.pallas_call(body, out_shape=jax.ShapeDtypeStruct((NZ, R0, C0), F32), i...  38.5 us
    unnamed x1, local copies, waits for them, and re-layouts  1.67 us

profile of v4, /device:TPU:24, one launch (start us, length us, event | category | flops | bytes accessed | tf_op | source)
XLA Modules:
  0.0 40.2 jit_solution(15704576344023797510)
XLA Ops:
  0.0 38.5 %shard_map.55 = f32[8,32,256]{2,1,0:T(8,128)} custom-call(f32[8,32,256]{2,1,0:T(8,128)} %refs_0_.1, bf16[8,32,256]{2,1,0:T(8,128)(2,1)} %refs_1_.1, bf16[8,32,256]{2,1,0:T(8,128)(2,1)} %refs_2_.1, bf16[8,32,256]{2,1,0:T(8,128)(2,1)} %refs_3_.1, bf16[8,32,256]{2,1,0:T(8,128)(2,1)} %refs_4_.1), custom_call_target="tpu_custom_call" | custom-call | tf_op jit(solution)/shard_map/pallas_call | solution.py:715
  38.5 1.7 %copy.7 = f32[8,32,256]{2,1,0:T(8,128)} copy(f32[8,32,256]{2,1,0:T(8,128)} %shard_map.55) | data formatting | bytes 524288

commit v5 on v4

--- a/solution.py
+++ b/solution.py
@@ -501,13 +501,6 @@
     l0.sweep(2, 31, l0.va, l0.vb)
     l0.restrict_residual(4, 30, l0.vb, l1)
     close = names("y1", [(0, 1), (0, -1)])
-    arrive(close)
-
-    def part1(e, dx, j):
-        return recv1[e, 1 - dx, 0], j
-
-    unpack(part1, l1.a, coefs, 8, 16, 8, 128, range(16))
-    l1.diagonal(1, 16)
     hear(1)
     tell(2)
     arrive(first[:3] + first[5:])
@@ -520,9 +513,17 @@
         l0.sweep(lo, hi, l0.va, l0.vb)
     for lo, hi in ((0, 4), (30, 32)):
         l0.restrict_residual(lo, hi, l0.vb, l1)
+    third = [("xr", 1), ("xr", -1)] + names("yr", sides)
+    send(third[:2])
     pack(l1.a, 0, 8, 16, 8, 0, sendr)
-    third = [("xr", 1), ("xr", -1)] + names("yr", sides)
-    send(third)
+    send(third[2:])
+    arrive(close)
+
+    def part1(e, dx, j):
+        return recv1[e, 1 - dx, 0], j
+
+    unpack(part1, l1.a, coefs, 8, 16, 8, 128, range(16))
+    l1.diagonal(1, 16)
     later = [("x0b", 1), ("x0c", 1), ("x0d", 1), ("x0b", -1)]
 
     arrive([n for n in second if n not in close])

time: 40.4 us -> 40.2 us (level)
  no operation moved by 1% of the time
where the time goes in v5:
time: 40.2 us; the launch traced here: 40.1 us
  Pallas kernels  38.4 us (96%)
  local copies, waits for them, and re-layouts  1.67 us (4%)
    pallas_call x1, Pallas kernels, step(): pl.pallas_call(body, out_shape=jax.ShapeDtypeStruct((NZ, R0, C0), F32), i...  38.4 us
    unnamed x1, local copies, waits for them, and re-layouts  1.67 us

profile of v5, /device:TPU:24, one launch (start us, length us, event | category | flops | bytes accessed | tf_op | source)
XLA Modules:
  0.0 40.1 jit_solution(17417510145753238119)
XLA Ops:
  0.0 38.4 %shard_map.55 = f32[8,32,256]{2,1,0:T(8,128)} custom-call(f32[8,32,256]{2,1,0:T(8,128)} %refs_0_.1, bf16[8,32,256]{2,1,0:T(8,128)(2,1)} %refs_1_.1, bf16[8,32,256]{2,1,0:T(8,128)(2,1)} %refs_2_.1, bf16[8,32,256]{2,1,0:T(8,128)(2,1)} %refs_3_.1, bf16[8,32,256]{2,1,0:T(8,128)(2,1)} %refs_4_.1), custom_call_target="tpu_custom_call" | custom-call | tf_op jit(solution)/shard_map/pallas_call | solution.py:716
  38.4 1.7 %copy.7 = f32[8,32,256]{2,1,0:T(8,128)} copy(f32[8,32,256]{2,1,0:T(8,128)} %shard_map.55) | data formatting | bytes 524288
